TPU v7x, 256 devices: a whole 4x4x8 slice. The times are simulated.
256 devices in a mesh: layer: 2 (over z_lo), latent: 32 (over x, y, core), token: 4 (over z_hi).
Axes of the slice: x: 4, y: 4, z: 8 (z_hi: 4, z_lo: 2; z = z_hi * 2 + z_lo), core: 2. Of those that a mesh axis runs over, the one named last changes fastest.
Arguments:
- resid_in: bfloat16 [2, 1024, 2304], P('layer', 'token', 'latent'), may hold values from -300 to 300
- clt_gain: float32 [2, 2304], P('layer'), may hold values from 0.1 to 1.9
- enc_w: bfloat16 [2, 2304, 16384], P('layer', None, 'latent'), may hold values from -0.125 to 0.125
- enc_b: float32 [2, 16384], P('layer', 'latent'), may hold values from -3 to 3
- dec_same: bfloat16 [2, 16384, 2304], P('layer', 'latent'), may hold values from -0.09375 to 0.09375
- dec_next: bfloat16 [16384, 2304], P('latent'), may hold values from -0.09375 to 0.09375
- frozen_sum: bfloat16 [1024, 2304], P('token', 'latent'), may hold values from -300 to 300
- mlp_gain: float32 [2304], P('latent'), may hold values from 0.1 to 1.9
- w_gate: bfloat16 [2304, 9216], P(None, ('layer', 'latent')), may hold values from -0.125 to 0.125
- w_up: bfloat16 [2304, 9216], P(None, ('layer', 'latent')), may hold values from -0.125 to 0.125
- w_down: bfloat16 [9216, 2304], P(('layer', 'latent')), may hold values from -0.1875 to 0.1875
Outputs:
- latents: bfloat16 [2, 1024, 16384], P('layer', 'token', 'latent')
- recon: bfloat16 [2, 1024, 2304], P('layer', 'token', 'latent')
- mlp_out: bfloat16 [1024, 2304], P('token', ('layer', 'latent'))
All inputs are finite; a program needn't handle non-finite values.
Results may differ from a plain program's by a relative error of at most 0.0074.
Values may be sent and summed in bfloat16 or wider, within the bound.
A program may use at most 64 MiB of HBM per device.

v0:
```python
import jax
import jax.numpy as jnp
from jax import lax
from jax.sharding import PartitionSpec as P

D = 2304


def in_order(tiles, dim):
    dims = list(tiles.shape[1:])
    dims[dim] *= tiles.shape[0]
    return jnp.moveaxis(tiles, 0, dim).reshape(dims)


def copy_for_each(value, axis):
    size = lax.axis_size(axis)
    return lax.all_to_all(
        jnp.broadcast_to(value[None], (size, *value.shape)), axis, 0, 0, tiled=True
    )


def gather_directly(value, axis, dim):
    return in_order(copy_for_each(value, axis), dim)


def passed_along(block, axis, distance):
    devices = range(lax.axis_size(axis))
    route = [(i - distance, i) for i in devices if i - distance in devices]
    return lax.ppermute(block, axis, route)


def split_up(value, dim, size):
    dims = value.shape
    tiles = value.reshape(*dims[:dim], size, dims[dim] // size, *dims[dim + 1 :])
    return jnp.moveaxis(tiles, dim, 0)


def summed_on_arrival(value, axis, dim):
    size = lax.axis_size(axis)
    tiles = lax.all_to_all(split_up(value, dim, size), axis, 0, 0, tiled=True)
    return jnp.sum(tiles, axis=0)


def swapped(value, axis, stride):
    mask = 2**stride
    pairs = [(source, source ^ mask) for source in range(lax.axis_size(axis))]
    return lax.ppermute(value, axis, pairs)


def over_copies(value, axis):
    return copy_for_each(value, axis).sum(axis=0)


def per_device(
    resid_in, clt_gain, enc_w, enc_b, dec_same, dec_next, frozen_sum, mlp_gain, w_gate, w_up, w_down
):
    own_rows = resid_in[0]
    gain_full = clt_gain[0]
    enc_local = enc_w[0]
    shard_piece = gather_directly(own_rows, "latent", 1)
    piece_values = shard_piece.astype(jnp.float32)
    gated = (shard_piece.astype(jnp.float32) * gain_full).astype(jnp.bfloat16)
    projected = jnp.dot(gated, enc_local, preferred_element_type=jnp.float32)
    squares = jnp.sum(piece_values * piece_values, axis=1, keepdims=True)
    inv_scale = lax.rsqrt(squares / D + 1e-06)
    lat_act = jnp.maximum(inv_scale * projected + enc_b[0], 0.0).astype(jnp.bfloat16)
    is_first = lax.axis_index("layer") == 0
    own_term = jnp.dot(lat_act, dec_same[0], preferred_element_type=jnp.float32)
    arrived = passed_along(lat_act, "layer", 1)
    target_term = own_term + jnp.dot(arrived, dec_next, preferred_element_type=jnp.float32)
    own_sum = summed_on_arrival(target_term, "latent", 1)
    other_sum = swapped(own_sum, "layer", 0)
    recon_zero = jnp.where(is_first, own_sum, other_sum)
    recon_one = jnp.where(is_first, other_sum, own_sum)
    recon = own_sum.astype(jnp.bfloat16)[None]
    mixed = frozen_sum.astype(jnp.float32) + recon_zero + recon_one
    normed = (mixed * mlp_gain).astype(jnp.bfloat16)
    mixed_squares = over_copies(jnp.sum(mixed * mixed, axis=1, keepdims=True), "latent")
    shard_piece = gather_directly(normed, "latent", 1)
    gate_raw = jnp.dot(shard_piece, w_gate, preferred_element_type=jnp.float32)
    up_raw = jnp.dot(shard_piece, w_up, preferred_element_type=jnp.float32)
    row_scale = lax.rsqrt(mixed_squares / D + 1e-06)
    hidden = (jax.nn.gelu(row_scale * gate_raw, approximate=True) * (row_scale * up_raw)).astype(
        jnp.bfloat16
    )
    partials = jnp.dot(hidden, w_down, preferred_element_type=jnp.float32)
    mlp_out = summed_on_arrival(partials, ("layer", "latent"), 1).astype(jnp.bfloat16)
    return (lat_act[None], recon, mlp_out)


def solution(mesh):
    in_specs = (
        P("layer", "token", "latent"),
        P("layer", None),
        P("layer", None, "latent"),
        P("layer", "latent"),
        P("layer", "latent", None),
        P("latent", None),
        P("token", "latent"),
        P("latent"),
        P(None, ("layer", "latent")),
        P(None, ("layer", "latent")),
        P(("layer", "latent"), None),
    )
    out_specs = (
        P("layer", "token", "latent"),
        P("layer", "token", "latent"),
        P("token", ("layer", "latent")),
    )
    return jax.shard_map(
        per_device, mesh=mesh, in_specs=in_specs, out_specs=out_specs, check_vma=False
    )
```

profile of v0, /device:TPU:1, one launch (start us, length us, event | category | flops | bytes accessed | tf_op | source)
XLA Modules:
  0.0 178.0 jit_solution(8213700717697507965)
XLA Ops:
  0.7 2.0 %broadcast_in_dim.11 = bf16[32,256,72]{1,2,0:T(8,128)(2,1)} broadcast(bf16[256,72]{0,1:T(8,128)(2,1)} %bitcast.46), dimensions={1,2} | broadcast | bytes 1216512 | tf_op jit(solution)/shard_map/broadcast_in_dim | solution.py:18
  2.7 8.6 %all-to-all-start = ((bf16[32,256,72]{1,2,0:T(8,128)(2,1)}), bf16[32,256,72]{1,2,0:T(8,128)(2,1)S(1)}, u32[]{:S(2)}, u32[]{:S(2)}) async-start(bf16[32,256,72]{1,2,0:T(8,128)(2,1)} %broadcast_in_dim.11), calls=%async_computation | async-start | bytes 2359296 | tf_op jit(solution)/shard_map/all_to_all | solution.py:17
  11.9 0.8 mul.76
  12.7 16.9 %all-to-all-done = bf16[32,256,72]{1,2,0:T(8,128)(2,1)S(1)} async-done(((bf16[32,256,72]{1,2,0:T(8,128)(2,1)}), bf16[32,256,72]{1,2,0:T(8,128)(2,1)S(1)}, u32[]{:S(2)}, u32[]{:S(2)}) %all-to-all-start) | async-done | bytes 1179680 | tf_op jit(solution)/shard_map/all_to_all | solution.py:17
  30.1 1.2 copy-done.6
  31.3 0.8 fusion.15
  32.1 3.8 %collective-permute-start = (bf16[256,512]{1,0:T(8,128)(2,1)S(1)}, bf16[256,512]{1,0:T(8,128)(2,1)S(1)}, u32[]{:S(2)}, u32[]{:S(2)}) collective-permute-start(bf16[256,512]{1,0:T(8,128)(2,1)S(1)} %fusion.15), channel_id=1, source_target_pairs={{0,128},{1,129},{2,130},{3,131},{4,132},{5,133},{6,134},{7,135},{8... | collective-permute-start | bytes 786440 | tf_op jit(solution)/shard_map/ppermute | solution.py:29
  36.7 4.6 %collective-permute-done = bf16[256,512]{1,0:T(8,128)(2,1)S(1)} collective-permute-done((bf16[256,512]{1,0:T(8,128)(2,1)S(1)}, bf16[256,512]{1,0:T(8,128)(2,1)S(1)}, u32[]{:S(2)}, u32[]{:S(2)}) %collective-permute-start) | collective-permute-done | bytes 262176 | tf_op jit(solution)/shard_map/ppermute | solution.py:29
  41.4 2.2 %convolution_add_fusion = f32[256,2304]{1,0:T(8,128)} fusion(f32[256,2304]{1,0:T(8,128)S(1)} %fusion.2, bf16[256,512]{1,0:T(8,128)(2,1)S(1)} %collective-permute-done, bf16[512,2304]{1,0:T(8,128)(2,1)S(1)} %copy-done.1), kind=kOutput, calls=%fused_computation | convolution fusion | flops 604569600 | bytes 7340032 | tf_op jit(solution)/shard_map/dot_general | solution.py:70
  43.5 3.1 %copy.18 = f32[256,2304]{0,1:T(8,128)} copy(f32[256,2304]{1,0:T(8,128)} %convolution_add_fusion) | data formatting | bytes 4718592 | tf_op jit(solution)/shard_map/add | solution.py:70
  46.6 37.1 %all_to_all.25 = f32[32,256,72]{1,2,0:T(8,128)} all-to-all(f32[32,256,72]{1,2,0:T(8,128)} %bitcast.43), channel_id=1, replica_groups=mesh['layer'=2,'latent'=32,'token'=4] {'latent'}, dimensions={0} | all-to-all | bytes 4718592 | tf_op jit(solution)/shard_map/all_to_all | solution.py:40
  83.7 1.8 %reduce_sum.46 = f32[256,72]{0,1:T(8,128)S(1)} reduce(f32[32,256,72]{1,2,0:T(8,128)} %all_to_all.25, f32[]{:T(128)} %constant.10.clone.1), dimensions={0}, to_apply=%region_1.0 | reduce | flops 571392 | bytes 2433028 | tf_op jit(solution)/shard_map/reduce_sum | solution.py:41
  85.5 2.3 %collective-permute-start.1 = (f32[256,72]{0,1:T(8,128)S(1)}, f32[256,72]{0,1:T(8,128)S(1)}, u32[]{:S(2)}, u32[]{:S(2)}) collective-permute-start(f32[256,72]{0,1:T(8,128)S(1)} %reduce_sum.46), channel_id=1, source_target_pairs={{0,128},{128,0},{1,129},{129,1},{2,130},{130,2},{3,131},{131,3},{4... | collective-permute-start | bytes 221192 | tf_op jit(solution)/shard_map/ppermute | solution.py:47
  87.8 2.5 %collective-permute-done.1 = f32[256,72]{0,1:T(8,128)S(1)} collective-permute-done((f32[256,72]{0,1:T(8,128)S(1)}, f32[256,72]{0,1:T(8,128)S(1)}, u32[]{:S(2)}, u32[]{:S(2)}) %collective-permute-start.1) | collective-permute-done | bytes 73760 | tf_op jit(solution)/shard_map/ppermute | solution.py:47
  91.0 11.4 %all_to_all.26 = f32[32,256,1]{1,2,0:T(1,128)} all-to-all(f32[32,256,1]{1,2,0:T(1,128)S(1)} %broadcast_in_dim.13), channel_id=1, replica_groups=mesh['layer'=2,'latent'=32,'token'=4] {'latent'}, dimensions={0} | all-to-all | bytes 65536 | tf_op jit(solution)/shard_map/all_to_all | solution.py:17
  102.4 1.1 broadcast_in_dim.28
  103.4 4.0 %all-to-all-start.3 = ((bf16[32,256,72]{1,2,0:T(8,128)(2,1)}), bf16[32,256,72]{1,2,0:T(8,128)(2,1)S(1)}, u32[]{:S(2)}, u32[]{:S(2)}) async-start(bf16[32,256,72]{1,2,0:T(8,128)(2,1)} %broadcast_in_dim.28), calls=%async_computation.3 | async-start | bytes 2359296 | tf_op jit(solution)/shard_map/all_to_all | solution.py:17
  107.4 0.8 reduce_sum.48
  108.3 17.6 %all-to-all-done.3 = bf16[32,256,72]{1,2,0:T(8,128)(2,1)S(1)} async-done(((bf16[32,256,72]{1,2,0:T(8,128)(2,1)}), bf16[32,256,72]{1,2,0:T(8,128)(2,1)S(1)}, u32[]{:S(2)}, u32[]{:S(2)}) %all-to-all-start.3) | async-done | bytes 1179680 | tf_op jit(solution)/shard_map/all_to_all | solution.py:17
  125.9 2.1 %fusion.27 = f32[256,144]{0,1:T(8,128)} fusion(bf16[2304,144]{0,1:T(8,128)(2,1)} %param.19, bf16[256,2304]{0,1:T(8,128)(2,1)S(1)} %bitcast.40, f32[256]{0:T(256)S(1)} %add_rsqrt_fusion), kind=kOutput, calls=%fused_computation.25 | convolution fusion | flops 170201088 | bytes 1991680 | tf_op jit(solution)/shard_map/dot_general | solution.py:80
  128.0 3.9 %fusion.20 = f32[256,2304]{0,1:T(8,128)} fusion(bf16[144,2304]{1,0:T(8,128)(2,1)} %param.21, f32[256,144]{0,1:T(8,128)} %fusion.27, bf16[2304,144]{0,1:T(8,128)(2,1)} %param.20, bf16[256,2304]{0,1:T(8,128)(2,1)S(1)} %bitcast.41, f32[256]{0:T(256)S(1)} %add_rsqrt_fusion), kind=kOutput, calls=%fused_computation.17 | convolution fusion | flops 339849216 | bytes 5014528 | tf_op jit(solution)/shard_map/dot_general | solution.py:86
  131.9 3.3 %reshape.54 = f32[256,64,36]{0,2,1:T(8,128)} reshape(f32[256,2304]{0,1:T(8,128)} %fusion.20) | data formatting | bytes 4718592 | tf_op jit(solution)/shard_map/reshape | solution.py:34
  135.3 40.2 %all_to_all.27 = f32[64,256,36]{1,2,0:T(8,128)} all-to-all(f32[64,256,36]{1,2,0:T(8,128)} %bitcast.42), channel_id=1, replica_groups=mesh['layer'=2,'latent'=32,'token'=4] {'layer','latent'}, dimensions={0} | all-to-all | bytes 4718592 | tf_op jit(solution)/shard_map/all_to_all | solution.py:40
  175.5 2.5 %reduce_sum.49 = bf16[256,36]{0,1:T(8,128)(2,1)} reduce(f32[64,256,36]{1,2,0:T(8,128)} %all_to_all.27, f32[]{:T(128)} %constant.10.clone.1), dimensions={0}, to_apply=%region_4.5 | reduce | flops 580608 | bytes 2377732 | tf_op jit(solution)/shard_map/reduce_sum | solution.py:41
  (22 shorter events, 2.6 us)
Async XLA Ops:
  0.6 35.3 %copy-start = (bf16[1,512,2304]{2,1,0:T(8,128)(2,1)S(1)}, bf16[1,512,2304]{2,1,0:T(8,128)(2,1)}, u32[]{:S(2)}) copy-start(bf16[1,512,2304]{2,1,0:T(8,128)(2,1)} %param.15) | copy-start | bytes 7077892
  0.6 10.6 %copy-start.4 = (f32[1,2304]{1,0:T(1,128)S(1)}, f32[1,2304]{1,0:T(1,128)}, u32[]{:S(2)}) copy-start(f32[1,2304]{1,0:T(1,128)} %param.12) | copy-start | bytes 27652
  2.7 27.0 %all-to-all-start = ((bf16[32,256,72]{1,2,0:T(8,128)(2,1)}), bf16[32,256,72]{1,2,0:T(8,128)(2,1)S(1)}, u32[]{:S(2)}, u32[]{:S(2)}) async-start(bf16[32,256,72]{1,2,0:T(8,128)(2,1)} %broadcast_in_dim.11), calls=%async_computation | async-start | bytes 2359296 | tf_op jit(solution)/shard_map/all_to_all | solution.py:17
  29.6 1.7 copy-start.6
  29.6 1.7 copy-start.7
  32.1 4.6 %copy-start.2 = (bf16[256,512]{1,0:T(8,128)(2,1)}, bf16[256,512]{1,0:T(8,128)(2,1)S(1)}, u32[]{:S(2)}) copy-start(bf16[256,512]{1,0:T(8,128)(2,1)S(1)} %fusion.15) | copy-start | bytes 786436
  32.1 9.3 %copy-start.1 = (bf16[512,2304]{1,0:T(8,128)(2,1)S(1)}, bf16[512,2304]{1,0:T(8,128)(2,1)}, u32[]{:S(2)}) copy-start(bf16[512,2304]{1,0:T(8,128)(2,1)} %param.16) | copy-start | bytes 7077892
  32.1 9.3 %collective-permute-start = (bf16[256,512]{1,0:T(8,128)(2,1)S(1)}, bf16[256,512]{1,0:T(8,128)(2,1)S(1)}, u32[]{:S(2)}, u32[]{:S(2)}) collective-permute-start(bf16[256,512]{1,0:T(8,128)(2,1)S(1)} %fusion.15), channel_id=1, source_target_pairs={{0,128},{1,129},{2,130},{3,131},{4,132},{5,133},{6,134},{7,135},{8... | collective-permute-start | bytes 786440 | tf_op jit(solution)/shard_map/ppermute | solution.py:29
  83.7 6.7 %copy-start.3 = (bf16[256,72]{0,1:T(8,128)(2,1)S(1)}, bf16[256,72]{0,1:T(8,128)(2,1)}, u32[]{:S(2)}) copy-start(bf16[256,72]{0,1:T(8,128)(2,1)} %param.17) | copy-start | bytes 110596
  83.7 6.7 %copy-start.5 = (f32[72]{0:T(128)S(1)}, f32[72]{0:T(128)}, u32[]{:S(2)}) copy-start(f32[72]{0:T(128)} %param.18) | copy-start | bytes 868
  85.5 4.8 %collective-permute-start.1 = (f32[256,72]{0,1:T(8,128)S(1)}, f32[256,72]{0,1:T(8,128)S(1)}, u32[]{:S(2)}, u32[]{:S(2)}) collective-permute-start(f32[256,72]{0,1:T(8,128)S(1)} %reduce_sum.46), channel_id=1, source_target_pairs={{0,128},{128,0},{1,129},{129,1},{2,130},{130,2},{3,131},{131,3},{4... | collective-permute-start | bytes 221192 | tf_op jit(solution)/shard_map/ppermute | solution.py:47
  103.4 22.4 %all-to-all-start.3 = ((bf16[32,256,72]{1,2,0:T(8,128)(2,1)}), bf16[32,256,72]{1,2,0:T(8,128)(2,1)S(1)}, u32[]{:S(2)}, u32[]{:S(2)}) async-start(bf16[32,256,72]{1,2,0:T(8,128)(2,1)} %broadcast_in_dim.28), calls=%async_computation.3 | async-start | bytes 2359296 | tf_op jit(solution)/shard_map/all_to_all | solution.py:17
where the time goes:
time: 179 us; the launch traced here: 178 us
  blocking collectives  88.6 us (49%)
  waiting for transfers between devices  41.7 us (23%)
  starting transfers between devices  18.7 us (10%)
  local copies, waits for them, and re-layouts  11.5 us (6%)
  matrix products  9.78 us (5%)
  other arithmetic  6.89 us (4%)
    all_to_all x2, blocking collectives, summed_on_arrival(): tiles = lax.all_to_all(split_up(value, dim, size), axis, 0, 0, tiled=True)  77.3 us
    all_to_all x2, waiting for transfers between devices, copy_for_each(): lax.all_to_all(jnp.broadcast_to(value[None], (size, *value.shape)), axis,...  34.6 us
    all_to_all x2, starting transfers between devices, copy_for_each(): lax.all_to_all(jnp.broadcast_to(value[None], (size, *value.shape)), axis,...  12.6 us
    all_to_all x1, blocking collectives, copy_for_each(): lax.all_to_all(jnp.broadcast_to(value[None], (size, *value.shape)), axis,...  11.4 us
    ppermute x1, waiting for transfers between devices, passed_along(): return lax.ppermute(block, axis, route)  4.62 us
    reduce_sum x2, other arithmetic, summed_on_arrival(): return jnp.sum(tiles, axis=0)  4.35 us
    dot_general x1, matrix products, per_device(): partials = jnp.dot(hidden, w_down, preferred_element_type=jnp.float32)  3.91 us
    ppermute x1, starting transfers between devices, passed_along(): return lax.ppermute(block, axis, route)  3.82 us
  transfers between devices with their start and end apart: 4, of which 4 were waited for; matrix products, arithmetic and copies ran while one was open for 2% of the time, Pallas kernels for 0%

commit v1 on v0

v1 whole, which is shorter than its diff:
```python
import jax
import jax.numpy as jnp
from jax import lax
from jax.experimental import pallas as pl
from jax.experimental.pallas import tpu as pltpu
from jax.sharding import PartitionSpec as P

D = 2304
TOK = 256
HALF = 128
CHIP = 144
OWN = 72
PAD = 80
LAT = 512
EPS = 1e-06
MESH = pl.DeviceIdType.MESH
F32 = jnp.float32
BF16 = jnp.bfloat16
TN = (((0,), (0,)), ((), ()))
NN = (((1,), (0,)), ((), ()))

SINGLES_A = [(1, 0), (3, 0), (2, 0)]
SINGLES_B = [(0, 1), (0, 3), (0, 2)]
DIAGONALS = [(1, 1), (3, 3), (1, 3), (3, 1), (1, 2), (2, 1), (3, 2), (2, 3), (2, 2)]
FAR_FIRST = [(a, b) for a in (2, 1, 3, 0) for b in (2, 1, 3, 0)]


def kernel(
    resid, gain, encb, frozen, mgain, enc, dec_s, dec_n, w_gate, w_up, w_down,
    lat_out, recon_out, mlp_out,
    resid_v, gain_v, encb_v, frozen_v, mgain_v, enc_v, dec_s_v, dec_n_v, wg_v, wu_v, wd_v,
    gain_b, encb_b, lb, g1, lat_v, lat_t,
    fz_send, fz_recv, mg_send, mg_recv,
    prod, ys, yr, keep, s1, r1, s2, r2,
    z_send, z_recv, rc_send, rc_recv, recon_v,
    sq_a, sq_b, sq_d, g2, fin_send, fin_recv, out_v,
    in_sem, ag_s, ag_r, d2_s, d2_r, rs_s, rs_d, rs_1, rs_2,
    ag2_s, ag2_r, ag2_d, sq_s, sq_r, ms_s, ms_r,
):
    layer = lax.axis_index("layer")
    q = lax.axis_index("latent")
    core = lax.rem(q, 2)
    chip = lax.div(q, 2)
    cy = lax.rem(chip, 4)
    cx = lax.div(chip, 4)
    first = core == 0

    def chip_at(a, b):
        dx = jnp.where(first, a, b)
        dy = jnp.where(first, b, a)
        return lax.rem(cx + dx, 4) * 4 + lax.rem(cy + dy, 4)

    def along_a(d):
        return {"latent": chip_at(d, 0) * 2 + core}

    def along_b(d):
        return {"latent": chip_at(0, d) * 2 + core}

    sibling = {"latent": chip * 2 + 1 - core}
    across = {"layer": 1 - layer}
    across_sib = {"layer": 1 - layer, "latent": chip * 2 + 1 - core}
    own_lanes = pl.ds(pl.multiple_of(core * HALF, HALF), HALF)
    sib_lanes = pl.ds(pl.multiple_of((1 - core) * HALF, HALF), HALF)

    sends = []

    def send(src, dst, ssem, rsem, dev):
        copy = pltpu.make_async_remote_copy(
            src_ref=src, dst_ref=dst, send_sem=ssem, recv_sem=rsem, device_id=dev, device_id_type=MESH
        )
        copy.start()
        return copy

    def arrived(dst, ssem, rsem):
        pltpu.make_async_remote_copy(
            src_ref=dst, dst_ref=dst, send_sem=ssem, recv_sem=rsem, device_id=sibling, device_id_type=MESH
        ).wait_recv()

    loads = [
        pltpu.make_async_copy(src, dst, in_sem.at[i])
        for i, (src, dst) in enumerate([
            (resid, resid_v), (gain, gain_v), (encb, encb_v), (frozen, frozen_v), (mgain, mgain_v),
            (enc, enc_v), (dec_s, dec_s_v), (dec_n, dec_n_v), (w_gate, wg_v), (w_up, wu_v), (w_down, wd_v),
        ])
    ]
    for copy in loads:
        copy.start()

    barrier = pltpu.get_barrier_semaphore()
    peers = [sibling, across, across_sib]
    peers += [along_a(d) for d in (1, 2, 3)] + [along_b(d) for d in (1, 2, 3)]
    for dev in peers:
        pl.semaphore_signal(barrier, inc=1, device_id=dev, device_id_type=MESH)
    loads[0].wait()
    lb[core, 0, 0:OWN, :] = resid_v[...]
    lb[core, 0, OWN:PAD, :] = jnp.zeros((PAD - OWN, TOK), BF16)
    pl.semaphore_wait(barrier, len(peers))

    def slot(a, b):
        return (a % 4) * 4 + b % 4

    def push(a, b, da, db):
        dev = along_a(da) if da else along_b(db)
        k = len(sends)
        sends.append(send(
            lb.at[core, slot(a, b)], lb.at[core, slot(a - da, b - db)],
            ag_s.at[k], ag_r.at[slot(a - da, b - db)], dev,
        ))

    def share(a, b):
        s = slot(a, b)
        sends.append(send(lb.at[core, s], lb.at[core, s], d2_s.at[s], d2_r.at[s], sibling))

    for d in (2, 1, 3):
        push(0, 0, d, 0)
    for d in (2, 1, 3):
        push(0, 0, 0, d)
    share(0, 0)

    for copy in loads[1:5]:
        copy.wait()
    for k in range(D // 128):
        gain_b[128 * k:128 * (k + 1), :] = jnp.broadcast_to(gain_v[:, 128 * k:128 * (k + 1)], (128, 128)).T
    for k in range(LAT // 128):
        encb_b[128 * k:128 * (k + 1), :] = jnp.broadcast_to(encb_v[:, 128 * k:128 * (k + 1)], (128, 128)).T
    mg_send[...] = jnp.broadcast_to(mgain_v[...], (128, OWN)).T
    fz_send[0:OWN, :] = frozen_v[:, sib_lanes]
    fz_send[OWN:PAD, :] = jnp.zeros((PAD - OWN, HALF), BF16)

    for a, b in SINGLES_A:
        arrived(lb.at[core, slot(a, b)], ag_s.at[0], ag_r.at[slot(a, b)])
        for d in (2, 1, 3):
            push(a, b, 0, d)
        share(a, b)
    sends.append(send(mg_send, mg_recv, ms_s.at[0], ms_r.at[0], sibling))
    sends.append(send(fz_send, fz_recv, ms_s.at[1], ms_r.at[1], sibling))

    squares = []

    def use(a, b):
        mirror = slot(b, a)
        arrived(lb.at[1 - core, mirror], ag_s.at[0], d2_r.at[mirror])
        slot0 = jnp.where(first, slot(a, b), mirror)
        slot1 = jnp.where(first, mirror, slot(a, b))
        rows = pl.ds(pl.multiple_of(chip_at(a, b) * CHIP, 16), CHIP)
        v = jnp.concatenate([lb[0, slot0, 0:OWN, :].astype(F32), lb[1, slot1, 0:OWN, :].astype(F32)], axis=0)
        squares.append(jnp.sum(v * v, axis=0, keepdims=True))
        g = gain_b[rows, :]
        g1[rows, :] = (v * jnp.concatenate([g, g], axis=1)).astype(BF16)

    use(0, 0)
    for a, b in SINGLES_B:
        arrived(lb.at[core, slot(a, b)], ag_s.at[0], ag_r.at[slot(a, b)])
        share(a, b)
    for a, b in SINGLES_A + SINGLES_B:
        use(a, b)
    pending = []
    for a, b in DIAGONALS:
        arrived(lb.at[core, slot(a, b)], ag_s.at[0], ag_r.at[slot(a, b)])
        share(a, b)
        pending.append((a, b))
        if (b, a) in pending:
            for pair in pending:
                use(*pair)
            pending = []
    total = squares[0]
    for s in squares[1:]:
        total = total + s
    inv = lax.rsqrt(total / D + EPS)

    loads[5].wait()
    pre = lax.dot_general(enc_v[...], g1[...], TN, preferred_element_type=F32)
    bias = encb_b[...]
    lat_v[...] = jnp.maximum(inv * pre + jnp.concatenate([bias, bias], axis=1), 0.0).astype(BF16)

    def project(dec_ref, i):
        for k in range(6):
            cols = slice(384 * k, 384 * (k + 1))
            prod[i, cols, :] = lax.dot_general(dec_ref[:, cols], lat_v[...], TN, preferred_element_type=F32)

    def whole_unit(i, c, lanes):
        rows = pl.ds(pl.multiple_of(c * CHIP, 16), CHIP)
        return prod[i, rows, lanes]

    def split_unit(i, c, lanes):
        low = pl.ds(pl.multiple_of(c * OWN, 8), OWN)
        high = pl.ds(pl.multiple_of(D // 2 + c * OWN, 8), OWN)
        return jnp.concatenate([prod[i, low, lanes], prod[i, high, lanes]], axis=0)

    def hand_over(i, unit):
        out = []
        for a, b in FAR_FIRST:
            s = slot(a, b)
            ys[i, s] = unit(i, chip_at(b, a), sib_lanes).astype(BF16)
            out.append(send(ys.at[i, s], yr.at[i, s], rs_s.at[i, s], rs_d.at[i, s], sibling))
        return out

    def first_axis(i, unit):
        out = []
        for a, b in FAR_FIRST:
            s = slot(a, b)
            arrived(yr.at[i, s], rs_s.at[i, 0], rs_d.at[i, s])
            v = unit(i, chip_at(a, b), own_lanes) + yr[i, s].astype(F32)
            if a:
                s1[i, s] = v.astype(BF16)
                t = slot(-a, b)
                out.append(send(s1.at[i, s], r1.at[i, t], rs_s.at[i, 16 + s], rs_1.at[i, t], along_a(a)))
            else:
                keep[i, b] = v
        return out

    def second_axis(i):
        out = []
        for b in (2, 1, 3, 0):
            v = keep[i, b]
            for a in (1, 3, 2):
                s = slot(a, b)
                arrived(r1.at[i, s], rs_s.at[i, 0], rs_1.at[i, s])
                v = v + r1[i, s].astype(F32)
            if b:
                s2[i, b] = v.astype(BF16)
                t = (4 - b) % 4
                out.append(send(s2.at[i, b], r2.at[i, t], rs_s.at[i, 16 + b], rs_2.at[i, t], along_b(b)))
            else:
                keep[i, 0] = v
        return out

    def collect(i):
        v = keep[i, 0]
        for b in (1, 3, 2):
            arrived(r2.at[i, b], rs_s.at[i, 0], rs_2.at[i, b])
            v = v + r2[i, b].astype(F32)
        return v

    def settle(copies):
        for copy in copies:
            copy.wait_send()

    loads[6].wait()
    loads[7].wait()

    @pl.when(layer == 0)
    def _():
        project(dec_n_v, 1)
        out = hand_over(1, whole_unit)
        project(dec_s_v, 0)
        out += hand_over(0, whole_unit)
        out += first_axis(1, whole_unit)
        out += first_axis(0, whole_unit)
        out += second_axis(1)
        out += second_axis(0)
        part = collect(1)
        keep[1, 0] = part
        z_send[1] = part.astype(BF16)
        out.append(send(z_send.at[1], z_recv.at[1], ms_s.at[3], ms_r.at[3], across))
        part = collect(0)
        keep[0, 0] = part
        z_send[0] = part.astype(BF16)
        out.append(send(z_send.at[0], z_recv.at[0], ms_s.at[2], ms_r.at[2], across))
        arrived(z_recv.at[0], ms_s.at[2], ms_r.at[2])
        keep[0, 1] = keep[1, 0] + z_recv[0].astype(F32)
        settle(out)

    @pl.when(layer == 1)
    def _():
        project(dec_s_v, 0)
        out = hand_over(0, whole_unit)
        out += first_axis(0, whole_unit)
        out += second_axis(0)
        part = collect(0)
        z_send[0] = part.astype(BF16)
        out.append(send(z_send.at[0], z_recv.at[0], ms_s.at[2], ms_r.at[2], across))
        arrived(z_recv.at[1], ms_s.at[3], ms_r.at[3])
        keep[0, 0] = part + z_recv[1].astype(F32)
        arrived(z_recv.at[0], ms_s.at[2], ms_r.at[2])
        keep[0, 1] = z_recv[0].astype(F32)
        settle(out)

    arrived(mg_recv, ms_s.at[0], ms_r.at[0])
    arrived(fz_recv, ms_s.at[1], ms_r.at[1])
    mine = frozen_v[:, own_lanes].astype(F32)
    theirs = fz_recv[0:OWN, :].astype(F32)
    fz = jnp.concatenate([jnp.where(first, mine, theirs), jnp.where(first, theirs, mine)], axis=0)
    mg0, mg1 = mg_send[...], mg_recv[...]
    mg = jnp.concatenate([jnp.where(first, mg0, mg1), jnp.where(first, mg1, mg0)], axis=0)
    mixed = fz + keep[0, 0] + keep[0, 1]

    sq_a[0] = jnp.broadcast_to(jnp.sum(mixed * mixed, axis=0, keepdims=True), (8, HALF))

    def block(a, b):
        return pl.ds(pl.multiple_of(chip_at(a, b) * CHIP, 16), CHIP)

    sends2 = []
    for d in (2, 1, 3):
        sends2.append(send(sq_a.at[0], sq_a.at[4 - d], sq_s.at[d], sq_r.at[4 - d], along_a(d)))
    g2[block(0, 0), own_lanes] = (mixed * mg).astype(BF16)

    def push2(a, b, da, db):
        dev = along_a(da) if da else along_b(db)
        ref = g2.at[block(a, b), own_lanes]
        sends2.append(send(ref, ref, ag2_s.at[len(sends2)], ag2_r.at[slot(a - da, b - db)], dev))

    def share2(a, b):
        ref = g2.at[block(a, b), own_lanes]
        sends2.append(send(ref, ref, ag2_s.at[len(sends2)], ag2_d.at[slot(a, b)], sibling))

    for d in (2, 1, 3):
        push2(0, 0, d, 0)
    for d in (2, 1, 3):
        push2(0, 0, 0, d)
    share2(0, 0)

    rows_own = keep[0, 0]
    low, high = rows_own[0:OWN], rows_own[OWN:CHIP]
    rc_send[0:OWN, :] = jnp.where(first, high, low).astype(BF16)
    rc_send[OWN:PAD, :] = jnp.zeros((PAD - OWN, HALF), BF16)
    sends2.append(send(rc_send, rc_recv, ms_s.at[4], ms_r.at[4], sibling))
    recon_v[:, own_lanes] = jnp.where(first, low, high).astype(BF16)
    lat_t[...] = lat_v[...].T
    lat_copy = pltpu.make_async_copy(lat_t, lat_out, in_sem.at[0])
    lat_copy.start()

    for a, b in SINGLES_A:
        arrived(g2.at[block(a, b), own_lanes], ag_s.at[0], ag2_r.at[slot(a, b)])
        for d in (2, 1, 3):
            push2(a, b, 0, d)
        share2(a, b)
    sq = sq_a[0]
    for d in (1, 3, 2):
        arrived(sq_a.at[d], ag_s.at[0], sq_r.at[d])
        sq = sq + sq_a[d]
    sq_b[0] = sq
    for d in (2, 1, 3):
        sends2.append(send(sq_b.at[0], sq_b.at[4 - d], sq_s.at[4 + d], sq_r.at[8 - d], along_b(d)))
    for a, b in SINGLES_B:
        arrived(g2.at[block(a, b), own_lanes], ag_s.at[0], ag2_r.at[slot(a, b)])
        share2(a, b)
    arrived(rc_recv, ms_s.at[4], ms_r.at[4])
    recon_v[:, sib_lanes] = rc_recv[0:OWN, :]
    recon_copy = pltpu.make_async_copy(recon_v, recon_out, in_sem.at[1])
    recon_copy.start()
    sq = sq_b[0]
    for d in (1, 3, 2):
        arrived(sq_b.at[d], ag_s.at[0], sq_r.at[4 + d])
        sq = sq + sq_b[d]
    sq_d[0] = sq
    sends2.append(send(sq_d.at[0], sq_d.at[1], sq_s.at[8], sq_r.at[8], sibling))
    for a, b in DIAGONALS:
        arrived(g2.at[block(a, b), own_lanes], ag_s.at[0], ag2_r.at[slot(a, b)])
        share2(a, b)
    arrived(sq_d.at[1], ag_s.at[0], sq_r.at[8])
    other = sq_d[1]
    both = jnp.concatenate([jnp.where(first, sq, other), jnp.where(first, other, sq)], axis=1)[0:1]
    scale = lax.rsqrt(both / D + EPS)
    for copy in loads[8:11]:
        copy.wait()
    for a in range(4):
        for b in range(4):
            arrived(g2.at[block(b, a), sib_lanes], ag_s.at[0], ag2_d.at[slot(a, b)])

    gate = scale * lax.dot_general(wg_v[...], g2[...], NN, preferred_element_type=F32)
    up = scale * lax.dot_general(wu_v[...], g2[...], NN, preferred_element_type=F32)
    hidden = (jax.nn.gelu(gate, approximate=True) * up).astype(BF16)
    for k in range(6):
        cols = slice(384 * k, 384 * (k + 1))
        prod[2, cols, :] = lax.dot_general(wd_v[:, cols], hidden, TN, preferred_element_type=F32)
    sends2 += hand_over(2, split_unit)
    sends2 += first_axis(2, split_unit)
    sends2 += second_axis(2)
    part = collect(2)
    low, high = part[0:OWN], part[OWN:CHIP]
    here = jnp.where(layer == 0, low, high)
    there = jnp.where(layer == 0, high, low)
    zero = jnp.zeros((PAD - OWN, HALF), BF16)
    fin_send[1, 0:OWN, :] = there.astype(BF16)
    fin_send[1, OWN:PAD, :] = zero
    sends2.append(send(fin_send.at[1], fin_recv.at[1], ms_s.at[5], ms_r.at[5], across_sib))
    sends2.append(send(fin_send.at[1], fin_recv.at[2], ms_s.at[6], ms_r.at[6], across))
    fin_send[0, 0:OWN, :] = here.astype(BF16)
    fin_send[0, OWN:PAD, :] = zero
    sends2.append(send(fin_send.at[0], fin_recv.at[0], ms_s.at[7], ms_r.at[7], sibling))
    arrived(fin_recv.at[0], ms_s.at[7], ms_r.at[7])
    arrived(fin_recv.at[2], ms_s.at[6], ms_r.at[6])
    arrived(fin_recv.at[1], ms_s.at[5], ms_r.at[5])
    own_half = here + fin_recv[2, 0:OWN, :].astype(F32)
    sib_half = fin_recv[0, 0:OWN, :].astype(F32) + fin_recv[1, 0:OWN, :].astype(F32)
    out_v[:, own_lanes] = jnp.where(first, own_half[0:36], own_half[36:72]).astype(BF16)
    out_v[:, sib_lanes] = jnp.where(first, sib_half[0:36], sib_half[36:72]).astype(BF16)
    out_copy = pltpu.make_async_copy(out_v, mlp_out, in_sem.at[2])
    out_copy.start()
    settle(sends)
    settle(sends2)
    lat_copy.wait()
    recon_copy.wait()
    out_copy.wait()


def per_device(
    resid_in, clt_gain, enc_w, enc_b, dec_same, dec_next, frozen_sum, mlp_gain, w_gate, w_up, w_down
):
    anywhere = pl.BlockSpec(memory_space=pl.ANY)
    dma = pltpu.SemaphoreType.DMA
    vm = pltpu.VMEM
    lat, recon, out = pl.pallas_call(
        kernel,
        out_shape=(
            jax.ShapeDtypeStruct((TOK, LAT), BF16),
            jax.ShapeDtypeStruct((OWN, TOK), BF16),
            jax.ShapeDtypeStruct((36, TOK), BF16),
        ),
        in_specs=[anywhere] * 11,
        out_specs=[anywhere] * 3,
        scratch_shapes=[
            vm((OWN, TOK), BF16), vm((1, D), F32), vm((1, LAT), F32), vm((OWN, TOK), BF16), vm((1, OWN), F32),
            vm((D, LAT), BF16), vm((LAT, D), BF16), vm((LAT, D), BF16),
            vm((CHIP, D), BF16), vm((CHIP, D), BF16), vm((CHIP, D), BF16),
            vm((D, HALF), F32), vm((LAT, HALF), F32), vm((2, 16, PAD, TOK), BF16), vm((D, TOK), BF16),
            vm((LAT, TOK), BF16), vm((TOK, LAT), BF16),
            vm((PAD, HALF), BF16), vm((PAD, HALF), BF16), vm((OWN, HALF), F32), vm((OWN, HALF), F32),
            vm((3, D, TOK), F32), vm((3, 16, CHIP, HALF), BF16), vm((3, 16, CHIP, HALF), BF16),
            vm((3, 4, CHIP, HALF), F32), vm((3, 16, CHIP, HALF), BF16), vm((3, 16, CHIP, HALF), BF16),
            vm((3, 4, CHIP, HALF), BF16), vm((3, 4, CHIP, HALF), BF16),
            vm((2, CHIP, HALF), BF16), vm((2, CHIP, HALF), BF16), vm((PAD, HALF), BF16), vm((PAD, HALF), BF16),
            vm((OWN, TOK), BF16),
            vm((4, 8, HALF), F32), vm((4, 8, HALF), F32), vm((2, 8, HALF), F32), vm((D, TOK), BF16),
            vm((2, PAD, HALF), BF16), vm((3, PAD, HALF), BF16), vm((36, TOK), BF16),
            dma((11,)), dma((32,)), dma((16,)), dma((16,)), dma((16,)),
            dma((3, 32)), dma((3, 16)), dma((3, 16)), dma((3, 4)),
            dma((48,)), dma((16,)), dma((16,)), dma((9,)), dma((9,)), dma((8,)), dma((8,)),
        ],
        compiler_params=pltpu.CompilerParams(
            collective_id=0, has_side_effects=True, vmem_limit_bytes=58 * 2**20
        ),
        cost_estimate=pl.CostEstimate(flops=2 * 10**9, bytes_accessed=10**7, transcendentals=0),
        name="clt_mlp",
    )(
        resid_in[0].T, clt_gain, enc_b, frozen_sum.T, mlp_gain[None],
        enc_w[0], dec_same[0], dec_next, w_gate.T, w_up.T, w_down,
    )
    return (lat[None], recon.T[None], out.T)


def solution(mesh):
    in_specs = (
        P("layer", "token", "latent"),
        P("layer", None),
        P("layer", None, "latent"),
        P("layer", "latent"),
        P("layer", "latent", None),
        P("latent", None),
        P("token", "latent"),
        P("latent"),
        P(None, ("layer", "latent")),
        P(None, ("layer", "latent")),
        P(("layer", "latent"), None),
    )
    out_specs = (
        P("layer", "token", "latent"),
        P("layer", "token", "latent"),
        P("token", ("layer", "latent")),
    )
    return jax.shard_map(
        per_device, mesh=mesh, in_specs=in_specs, out_specs=out_specs, check_vma=False
    )
```

time: 179 us -> 74 us (0.41)
  blocking collectives: 88.6 us -> 0 us
  Pallas kernels: 0 us -> 68.7 us
  waiting for transfers between devices: 41.7 us -> 0 us
  starting transfers between devices: 18.7 us -> 0 us
  matrix products: 9.78 us -> 0 us
  local copies, waits for them, and re-layouts: 11.5 us -> 4.39 us
  other arithmetic: 6.89 us -> 0 us
    all_to_all x3 -> x0, blocking collectives: 88.6 us -> none  [the longest x2 77.3 us: summed_on_arrival(): tiles = lax.all_to_all(split_up(value, dim, size), axis, 0, 0, tiled=True)]
    pallas_call x0 -> x1, Pallas kernels: none -> 68.7 us  [per_device(): pl.pallas_call(kernel, out_shape=(jax.ShapeDtypeStruct((TOK, LAT), BF16),...]
    all_to_all x2 -> x0, waiting for transfers between devices: 34.6 us -> none  [copy_for_each(): lax.all_to_all(jnp.broadcast_to(value[None], (size, *value.shape)), axis,...]
    all_to_all x2 -> x0, starting transfers between devices: 12.6 us -> none  [copy_for_each(): lax.all_to_all(jnp.broadcast_to(value[None], (size, *value.shape)), axis,...]
    dot_general x5 -> x0, matrix products: 9.78 us -> none  [the longest x1 3.91 us: per_device(): partials = jnp.dot(hidden, w_down, preferred_element_type=jnp.float32)]
    ppermute x2 -> x0, waiting for transfers between devices: 7.17 us -> none  [the longest x1 4.62 us: passed_along(): return lax.ppermute(block, axis, route)]
    reduce_sum x5 -> x0, other arithmetic: 6.24 us -> none  [the longest x2 4.35 us: summed_on_arrival(): return jnp.sum(tiles, axis=0)]
    ppermute x2 -> x0, starting transfers between devices: 6.11 us -> none  [the longest x1 3.82 us: passed_along(): return lax.ppermute(block, axis, route)]
  transfers between devices with their start and end apart: 4 -> 0, of which waited for: 4 -> 0; matrix products, arithmetic and copies ran while one was open for 2% -> 0% of each run, Pallas kernels for 0% -> 0%
where the time goes in v1:
time: 74 us; the launch traced here: 73.7 us
  Pallas kernels  68.7 us (93%)
  local copies, waits for them, and re-layouts  4.39 us (6%)
    pallas_call x1, Pallas kernels, per_device(): pl.pallas_call(kernel, out_shape=(jax.ShapeDtypeStruct((TOK, LAT), BF16),...  68.7 us
    unnamed x3, local copies, waits for them, and re-layouts  4.39 us

profile of v1, /device:TPU:1, one launch (start us, length us, event | category | flops | bytes accessed | tf_op | source)
XLA Modules:
  0.0 73.7 jit_solution(11780350363926383886)
XLA Ops:
  0.6 68.7 %clt_mlp.1 = (bf16[256,512]{1,0:T(8,128)(2,1)}, bf16[72,256]{1,0:T(8,128)(2,1)}, bf16[36,256]{1,0:T(8,128)(2,1)}) custom-call(bf16[72,256]{1,0:T(8,128)(2,1)} %bitcast.19, f32[1,2304]{1,0:T(1,128)} %gain.1, f32[1,512]{1,0:T(1,128)} %encb.1, bf16[72,256]{1,0:T(8,128)(2,1)} %bitcast.20, f32[1,72]{1,0:T(1,128)} %bitcast.23, bf16[2304,512]{1,0:T(8,128)(2,1)} %bitcast.14, ...), custom_call_target="tpu_custom_call" | custom-call | flops 2000000000 | bytes 10000000 | tf_op jit(solution)/shard_map/clt_mlp/pallas_call | solution.py:404
  69.3 1.7 %copy.17 = bf16[1,256,512]{2,1,0:T(8,128)(2,1)} copy(bf16[1,256,512]{2,1,0:T(8,128)(2,1)} %bitcast.18) | data formatting | bytes 524288
  71.0 1.4 %copy.18 = bf16[1,256,72]{1,2,0:T(8,128)(2,1)} copy(bf16[1,256,72]{1,2,0:T(8,128)(2,1)} %bitcast.21) | data formatting | bytes 73728
  72.4 1.3 %copy.19 = bf16[256,36]{0,1:T(8,128)(2,1)} copy(bf16[256,36]{0,1:T(8,128)(2,1)} %bitcast.22) | data formatting | bytes 36864

commit v2 on v1

v2 whole, which is shorter than its diff:
```python
import jax
import jax.numpy as jnp
from jax import lax
from jax.experimental import pallas as pl
from jax.experimental.pallas import tpu as pltpu
from jax.sharding import PartitionSpec as P

D = 2304
TOK = 256
HALF = 128
CHIP = 144
OWN = 72
PAD = 80
LAT = 512
EPS = 1e-06
MESH = pl.DeviceIdType.MESH
F32 = jnp.float32
BF16 = jnp.bfloat16
TN = (((0,), (0,)), ((), ()))
NN = (((1,), (0,)), ((), ()))

SINGLES_A = [(1, 0), (3, 0), (2, 0)]
SINGLES_B = [(0, 1), (0, 3), (0, 2)]
DIAGONALS = [(1, 1), (3, 3), (1, 3), (3, 1), (1, 2), (2, 1), (3, 2), (2, 3), (2, 2)]
FAR_FIRST = [(a, b) for a in (2, 1, 3, 0) for b in (2, 1, 3, 0)]


def kernel(
    resid, gain, encb, frozen, mgain, enc, dec_s, dec_n, w_gate, w_up, w_down,
    lat_out, recon_out, mlp_out,
    resid_v, gain_v, encb_v, frozen_v, mgain_v, enc_v, dec_s_v, dec_n_v, wg_v, wu_v, wd_v,
    gain_b, encb_b, lb, g1, lat_v, lat_t,
    fz_send, fz_recv, mg_send, mg_recv,
    prod, ys, land, keep, s1, s2,
    z_send, z_recv, rc_send, rc_recv, recon_v,
    sq_all, sq_a, sq_b, sq_d, g2, fin_send, fin_recv, out_v,
    in_sem, out_sem, ag_r, ag_d, rs_s, rs_d, rs_1, rs_2, sq_r, ms_s, ms_r,
):
    layer = lax.axis_index("layer")
    q = lax.axis_index("latent")
    core = lax.rem(q, 2)
    chip = lax.div(q, 2)
    cy = lax.rem(chip, 4)
    cx = lax.div(chip, 4)
    first = core == 0

    def chip_at(a, b):
        dx = jnp.where(first, a, b)
        dy = jnp.where(first, b, a)
        return lax.rem(cx + dx, 4) * 4 + lax.rem(cy + dy, 4)

    def along_a(d):
        return {"latent": chip_at(d, 0) * 2 + core}

    def along_b(d):
        return {"latent": chip_at(0, d) * 2 + core}

    sibling = {"latent": chip * 2 + 1 - core}
    across = {"layer": 1 - layer}
    across_sib = {"layer": 1 - layer, "latent": chip * 2 + 1 - core}
    own_lanes = pl.ds(pl.multiple_of(core * HALF, HALF), HALF)
    sib_lanes = pl.ds(pl.multiple_of((1 - core) * HALF, HALF), HALF)

    def send(src, dst, ssem, rsem, dev):
        copy = pltpu.make_async_remote_copy(
            src_ref=src, dst_ref=dst, send_sem=ssem, recv_sem=rsem, device_id=dev, device_id_type=MESH
        )
        copy.start()
        return copy

    def arrived(dst, rsem):
        pltpu.make_async_remote_copy(
            src_ref=dst, dst_ref=dst, send_sem=out_sem.at[0], recv_sem=rsem, device_id=sibling, device_id_type=MESH
        ).wait_recv()

    def all_sent(refs, ssem):
        pltpu.make_async_remote_copy(
            src_ref=refs, dst_ref=refs, send_sem=ssem, recv_sem=ag_r.at[0, 0], device_id=sibling, device_id_type=MESH
        ).wait_send()

    loads = [
        pltpu.make_async_copy(src, dst, in_sem.at[i])
        for i, (src, dst) in enumerate([
            (resid, resid_v), (gain, gain_v), (encb, encb_v), (frozen, frozen_v), (mgain, mgain_v),
            (enc, enc_v), (dec_s, dec_s_v), (dec_n, dec_n_v), (w_gate, wg_v), (w_up, wu_v), (w_down, wd_v),
        ])
    ]
    for copy in loads:
        copy.start()

    barrier = pltpu.get_barrier_semaphore()
    peers = [sibling, across, across_sib]
    peers += [along_a(d) for d in (1, 2, 3)] + [along_b(d) for d in (1, 2, 3)]
    for dev in peers:
        pl.semaphore_signal(barrier, inc=1, device_id=dev, device_id_type=MESH)
    loads[0].wait()
    lb[core * 16, 0:OWN, :] = resid_v[...]
    lb[core * 16, OWN:PAD, :] = jnp.zeros((PAD - OWN, TOK), BF16)
    pl.semaphore_wait(barrier, len(peers))

    def slot(a, b):
        return (a % 4) * 4 + b % 4

    def group(a, b):
        a, b = a % 4, b % 4
        return a - 1 if b == 0 else 3 + a

    def push(a, b, da, db):
        dev = along_a(da) if da else along_b(db)
        send(
            lb.at[core * 16 + slot(a, b)], lb.at[core * 16 + slot(a - da, b - db)],
            out_sem.at[0], ag_r.at[0, group(a - da, b - db)], dev,
        )

    def share(a, b, n, k):
        ref = lb.at[pl.ds(core * 16 + slot(a, b), n)]
        send(ref, ref, out_sem.at[0], ag_d.at[0, k], sibling)

    for d in (2, 1, 3):
        push(0, 0, d, 0)
    for d in (2, 1, 3):
        push(0, 0, 0, d)
    share(0, 0, 1, 0)

    for copy in loads[1:5]:
        copy.wait()
    for k in range(D // 128):
        gain_b[128 * k:128 * (k + 1), :] = jnp.broadcast_to(gain_v[:, 128 * k:128 * (k + 1)], (128, 128)).T
    for k in range(LAT // 128):
        encb_b[128 * k:128 * (k + 1), :] = jnp.broadcast_to(encb_v[:, 128 * k:128 * (k + 1)], (128, 128)).T
    mg_send[...] = jnp.broadcast_to(mgain_v[...], (128, OWN)).T
    fz_send[0:OWN, :] = frozen_v[:, sib_lanes]
    fz_send[OWN:PAD, :] = jnp.zeros((PAD - OWN, HALF), BF16)

    for a, b in SINGLES_A:
        arrived(lb.at[core * 16 + slot(a, b)], ag_r.at[0, group(a, b)])
        for d in (2, 1, 3):
            push(a, b, 0, d)
        share(a, b, 1, a)
    sends = [
        send(mg_send, mg_recv, ms_s.at[0], ms_r.at[0], sibling),
        send(fz_send, fz_recv, ms_s.at[1], ms_r.at[1], sibling),
    ]

    squares = []

    def use(a, b):
        mine, mirror = slot(a, b), slot(b, a)
        slot0 = jnp.where(first, mine, mirror)
        slot1 = jnp.where(first, mirror, mine)
        rows = pl.ds(pl.multiple_of(chip_at(a, b) * CHIP, 16), CHIP)
        v = jnp.concatenate([lb[slot0, 0:OWN, :].astype(F32), lb[16 + slot1, 0:OWN, :].astype(F32)], axis=0)
        squares.append(jnp.sum(v * v, axis=0, keepdims=True))
        g = gain_b[rows, :]
        g1[rows, :] = (v * jnp.concatenate([g, g], axis=1)).astype(BF16)

    def shared(a, b, n, k):
        arrived(lb.at[pl.ds((1 - core) * 16 + slot(a, b), n)], ag_d.at[0, k])

    shared(0, 0, 1, 0)
    use(0, 0)
    arrived(lb.at[pl.ds(core * 16 + 1, 3)], ag_r.at[0, 3])
    share(0, 1, 3, 4)
    shared(0, 1, 3, 4)
    for a, b in SINGLES_A:
        use(a, b)
    for a, b in SINGLES_A:
        shared(a, b, 1, a)
    for a, b in SINGLES_B:
        use(a, b)
    for a in (1, 3, 2):
        arrived(lb.at[pl.ds(core * 16 + slot(a, 1), 3)], ag_r.at[0, 3 + a])
        share(a, 1, 3, 4 + a)
    for a in (1, 3, 2):
        shared(a, 1, 3, 4 + a)
    for a, b in DIAGONALS:
        use(a, b)
    total = squares[0]
    for s in squares[1:]:
        total = total + s
    inv = lax.rsqrt(total / D + EPS)

    loads[5].wait()
    pre = lax.dot_general(enc_v[...], g1[...], TN, preferred_element_type=F32)
    bias = encb_b[...]
    lat_v[...] = jnp.maximum(inv * pre + jnp.concatenate([bias, bias], axis=1), 0.0).astype(BF16)

    def project(dec_ref, i):
        for k in range(6):
            cols = slice(384 * k, 384 * (k + 1))
            prod[i, cols, :] = lax.dot_general(dec_ref[:, cols], lat_v[...], TN, preferred_element_type=F32)

    def whole_unit(i, c, lanes):
        rows = pl.ds(pl.multiple_of(c * CHIP, 16), CHIP)
        return prod[i, rows, lanes]

    def split_unit(i, c, lanes):
        low = pl.ds(pl.multiple_of(c * OWN, 8), OWN)
        high = pl.ds(pl.multiple_of(D // 2 + c * OWN, 8), OWN)
        return jnp.concatenate([prod[i, low, lanes], prod[i, high, lanes]], axis=0)

    def hand_over(i, unit):
        for a in (2, 1, 3, 0):
            for b in range(4):
                ys[i, slot(a, b)] = unit(i, chip_at(b, a), sib_lanes).astype(BF16)
            send(ys.at[i, 4 * a:4 * a + 4], land.at[i, 4 * a:4 * a + 4], rs_s.at[i], rs_d.at[i, a], sibling)

    def first_axis(i, unit):
        for a in (2, 1, 3, 0):
            arrived(land.at[i, 4 * a:4 * a + 4], rs_d.at[i, a])
            for b in (2, 1, 3, 0):
                s = slot(a, b)
                v = unit(i, chip_at(a, b), own_lanes) + land[i, s].astype(F32)
                if a:
                    s1[i, s] = v.astype(BF16)
                    send(s1.at[i, s], land.at[i, 16 + 3 * b + 3 - a], rs_s.at[i], rs_1.at[i, b], along_a(a))
                else:
                    keep[i, b] = v

    def second_axis(i):
        for b in (2, 1, 3, 0):
            at = 16 + 3 * b
            arrived(land.at[i, at:at + 3], rs_1.at[i, b])
            v = keep[i, b] + land[i, at].astype(F32) + land[i, at + 1].astype(F32) + land[i, at + 2].astype(F32)
            if b:
                s2[i, b] = v.astype(BF16)
                send(s2.at[i, b], land.at[i, 28 + 3 - b], rs_s.at[i], rs_2.at[i], along_b(b))
            else:
                keep[i, 0] = v

    def collect(i):
        arrived(land.at[i, 28:31], rs_2.at[i])
        return keep[i, 0] + land[i, 28].astype(F32) + land[i, 29].astype(F32) + land[i, 30].astype(F32)

    def settle(copies):
        for copy in copies:
            copy.wait_send()

    loads[6].wait()
    loads[7].wait()

    @pl.when(layer == 0)
    def _():
        project(dec_n_v, 1)
        hand_over(1, whole_unit)
        project(dec_s_v, 0)
        hand_over(0, whole_unit)
        first_axis(1, whole_unit)
        first_axis(0, whole_unit)
        second_axis(1)
        second_axis(0)
        part = collect(1)
        keep[1, 0] = part
        z_send[1] = part.astype(BF16)
        early = send(z_send.at[1], z_recv.at[1], ms_s.at[3], ms_r.at[3], across)
        part = collect(0)
        keep[0, 0] = part
        z_send[0] = part.astype(BF16)
        last = send(z_send.at[0], z_recv.at[0], ms_s.at[2], ms_r.at[2], across)
        arrived(z_recv.at[0], ms_r.at[2])
        keep[0, 1] = keep[1, 0] + z_recv[0].astype(F32)
        all_sent(land.at[1, 0:31], rs_s.at[1])
        all_sent(land.at[0, 0:31], rs_s.at[0])
        settle([early, last])

    @pl.when(layer == 1)
    def _():
        project(dec_s_v, 0)
        hand_over(0, whole_unit)
        first_axis(0, whole_unit)
        second_axis(0)
        part = collect(0)
        z_send[0] = part.astype(BF16)
        last = send(z_send.at[0], z_recv.at[0], ms_s.at[2], ms_r.at[2], across)
        arrived(z_recv.at[1], ms_r.at[3])
        keep[0, 0] = part + z_recv[1].astype(F32)
        arrived(z_recv.at[0], ms_r.at[2])
        keep[0, 1] = z_recv[0].astype(F32)
        all_sent(land.at[0, 0:31], rs_s.at[0])
        settle([last])

    arrived(mg_recv, ms_r.at[0])
    arrived(fz_recv, ms_r.at[1])
    mine = frozen_v[:, own_lanes].astype(F32)
    theirs = fz_recv[0:OWN, :].astype(F32)
    fz = jnp.concatenate([jnp.where(first, mine, theirs), jnp.where(first, theirs, mine)], axis=0)
    mg0, mg1 = mg_send[...], mg_recv[...]
    mg = jnp.concatenate([jnp.where(first, mg0, mg1), jnp.where(first, mg1, mg0)], axis=0)
    mixed = fz + keep[0, 0] + keep[0, 1]

    sq_a[0] = jnp.broadcast_to(jnp.sum(mixed * mixed, axis=0, keepdims=True), (8, HALF))

    def block(a, b):
        return pl.ds(pl.multiple_of(chip_at(a, b) * CHIP, 16), CHIP)

    sends2 = []
    for d in (2, 1, 3):
        send(sq_a.at[0], sq_a.at[4 - d], out_sem.at[2], sq_r.at[0], along_a(d))
    g2[block(0, 0), own_lanes] = (mixed * mg).astype(BF16)

    def push2(a, b, da, db):
        dev = along_a(da) if da else along_b(db)
        ref = g2.at[block(a, b), own_lanes]
        send(ref, ref, out_sem.at[1], ag_r.at[1, group(a - da, b - db)], dev)

    def share2(a, b, k):
        ref = g2.at[block(a, b), own_lanes]
        send(ref, ref, out_sem.at[1], ag_d.at[1, k], sibling)

    three = land.at[0, 28:31]

    for d in (2, 1, 3):
        push2(0, 0, d, 0)
    for d in (2, 1, 3):
        push2(0, 0, 0, d)
    share2(0, 0, 0)

    rows_own = keep[0, 0]
    low, high = rows_own[0:OWN], rows_own[OWN:CHIP]
    rc_send[0:OWN, :] = jnp.where(first, high, low).astype(BF16)
    rc_send[OWN:PAD, :] = jnp.zeros((PAD - OWN, HALF), BF16)
    sends2.append(send(rc_send, rc_recv, ms_s.at[4], ms_r.at[4], sibling))
    recon_v[:, own_lanes] = jnp.where(first, low, high).astype(BF16)
    lat_t[...] = lat_v[...].T
    lat_copy = pltpu.make_async_copy(lat_t, lat_out, in_sem.at[0])
    lat_copy.start()

    for a, b in SINGLES_A:
        arrived(g2.at[block(a, b), own_lanes], ag_r.at[1, group(a, b)])
        for d in (2, 1, 3):
            push2(a, b, 0, d)
        share2(a, b, a)
    arrived(sq_a.at[1:4], sq_r.at[0])
    sq = sq_a[0] + sq_a[1] + sq_a[2] + sq_a[3]
    sq_b[0] = sq
    for d in (2, 1, 3):
        send(sq_b.at[0], sq_b.at[4 - d], out_sem.at[2], sq_r.at[1], along_b(d))
    arrived(three, ag_r.at[1, 3])
    for a, b in SINGLES_B:
        share2(a, b, 4)
    arrived(rc_recv, ms_r.at[4])
    recon_v[:, sib_lanes] = rc_recv[0:OWN, :]
    recon_copy = pltpu.make_async_copy(recon_v, recon_out, in_sem.at[1])
    recon_copy.start()
    arrived(sq_b.at[1:4], sq_r.at[1])
    sq = sq_b[0] + sq_b[1] + sq_b[2] + sq_b[3]
    sq_d[0] = sq
    send(sq_d.at[0], sq_d.at[1], out_sem.at[2], sq_r.at[2], sibling)
    for a in (1, 3, 2):
        arrived(three, ag_r.at[1, 3 + a])
        for b in (1, 3, 2):
            share2(a, b, 4 + a)
    arrived(sq_d.at[1], sq_r.at[2])
    other = sq_d[1]
    both = jnp.concatenate([jnp.where(first, sq, other), jnp.where(first, other, sq)], axis=1)[0:1]
    scale = lax.rsqrt(both / D + EPS)
    for copy in loads[8:11]:
        copy.wait()
    for k in range(4):
        arrived(land.at[0, 28], ag_d.at[1, k])
    for k in range(4, 8):
        arrived(three, ag_d.at[1, k])

    gate = scale * lax.dot_general(wg_v[...], g2[...], NN, preferred_element_type=F32)
    up = scale * lax.dot_general(wu_v[...], g2[...], NN, preferred_element_type=F32)
    hidden = (jax.nn.gelu(gate, approximate=True) * up).astype(BF16)
    for k in range(6):
        cols = slice(384 * k, 384 * (k + 1))
        prod[2, cols, :] = lax.dot_general(wd_v[:, cols], hidden, TN, preferred_element_type=F32)
    hand_over(2, split_unit)
    first_axis(2, split_unit)
    second_axis(2)
    part = collect(2)
    low, high = part[0:OWN], part[OWN:CHIP]
    here = jnp.where(layer == 0, low, high)
    there = jnp.where(layer == 0, high, low)
    zero = jnp.zeros((PAD - OWN, HALF), BF16)
    fin_send[1, 0:OWN, :] = there.astype(BF16)
    fin_send[1, OWN:PAD, :] = zero
    sends2.append(send(fin_send.at[1], fin_recv.at[1], ms_s.at[5], ms_r.at[5], across_sib))
    sends2.append(send(fin_send.at[1], fin_recv.at[2], ms_s.at[6], ms_r.at[6], across))
    fin_send[0, 0:OWN, :] = here.astype(BF16)
    fin_send[0, OWN:PAD, :] = zero
    sends2.append(send(fin_send.at[0], fin_recv.at[0], ms_s.at[7], ms_r.at[7], sibling))
    arrived(fin_recv.at[0], ms_r.at[7])
    arrived(fin_recv.at[2], ms_r.at[6])
    arrived(fin_recv.at[1], ms_r.at[5])
    own_half = here + fin_recv[2, 0:OWN, :].astype(F32)
    sib_half = fin_recv[0, 0:OWN, :].astype(F32) + fin_recv[1, 0:OWN, :].astype(F32)
    out_v[:, own_lanes] = jnp.where(first, own_half[0:36], own_half[36:72]).astype(BF16)
    out_v[:, sib_lanes] = jnp.where(first, sib_half[0:36], sib_half[36:72]).astype(BF16)
    out_copy = pltpu.make_async_copy(out_v, mlp_out, in_sem.at[2])
    out_copy.start()
    all_sent(lb.at[0:31], out_sem.at[0])
    all_sent(land.at[0, 0:31], out_sem.at[1])
    all_sent(sq_all, out_sem.at[2])
    all_sent(land.at[2, 0:31], rs_s.at[2])
    settle(sends)
    settle(sends2)
    lat_copy.wait()
    recon_copy.wait()
    out_copy.wait()


def write_out(lat, recon, out, lat_out, recon_out, mlp_out, sem):
    copies = [
        pltpu.make_async_copy(src, dst, sem.at[i])
        for i, (src, dst) in enumerate([(lat, lat_out), (recon, recon_out), (out, mlp_out)])
    ]
    for copy in copies:
        copy.start()
    for copy in copies:
        copy.wait()


def per_device(
    resid_in, clt_gain, enc_w, enc_b, dec_same, dec_next, frozen_sum, mlp_gain, w_gate, w_up, w_down
):
    anywhere = pl.BlockSpec(memory_space=pl.ANY)
    dma = pltpu.SemaphoreType.DMA
    vm = pltpu.VMEM
    lat, recon, out = pl.pallas_call(
        kernel,
        out_shape=(
            jax.ShapeDtypeStruct((TOK, LAT), BF16),
            jax.ShapeDtypeStruct((OWN, TOK), BF16),
            jax.ShapeDtypeStruct((36, TOK), BF16),
        ),
        in_specs=[anywhere] * 11,
        out_specs=[anywhere] * 3,
        scratch_shapes=[
            vm((OWN, TOK), BF16), vm((1, D), F32), vm((1, LAT), F32), vm((OWN, TOK), BF16), vm((1, OWN), F32),
            vm((D, LAT), BF16), vm((LAT, D), BF16), vm((LAT, D), BF16),
            vm((CHIP, D), BF16), vm((CHIP, D), BF16), vm((CHIP, D), BF16),
            vm((D, HALF), F32), vm((LAT, HALF), F32), vm((32, PAD, TOK), BF16), vm((D, TOK), BF16),
            vm((LAT, TOK), BF16), vm((TOK, LAT), BF16),
            vm((PAD, HALF), BF16), vm((PAD, HALF), BF16), vm((OWN, HALF), F32), vm((OWN, HALF), F32),
            vm((3, D, TOK), F32), vm((3, 16, CHIP, HALF), BF16), vm((3, 31, CHIP, HALF), BF16),
            vm((3, 4, CHIP, HALF), F32), vm((3, 16, CHIP, HALF), BF16), vm((3, 4, CHIP, HALF), BF16),
            vm((2, CHIP, HALF), BF16), vm((2, CHIP, HALF), BF16), vm((PAD, HALF), BF16), vm((PAD, HALF), BF16),
            vm((OWN, TOK), BF16),
            vm((7, 8, HALF), F32), vm((4, 8, HALF), F32), vm((4, 8, HALF), F32), vm((2, 8, HALF), F32), vm((D, TOK), BF16),
            vm((2, PAD, HALF), BF16), vm((3, PAD, HALF), BF16), vm((36, TOK), BF16),
            dma((11,)), dma((3,)), dma((2, 7)), dma((2, 8)),
            dma((3,)), dma((3, 4)), dma((3, 4)), dma((3,)), dma((3,)), dma((8,)), dma((8,)),
        ],
        compiler_params=pltpu.CompilerParams(
            collective_id=0, has_side_effects=True, vmem_limit_bytes=58 * 2**20
        ),
        cost_estimate=pl.CostEstimate(flops=2 * 10**9, bytes_accessed=10**7, transcendentals=0),
        name="clt_mlp",
    )(
        resid_in[0].T, clt_gain, enc_b, frozen_sum.T, mlp_gain[None],
        enc_w[0], dec_same[0], dec_next, w_gate.T, w_up.T, w_down,
    )
    lat, recon, out = pl.pallas_call(
        write_out,
        out_shape=(
            jax.ShapeDtypeStruct((TOK, LAT), BF16),
            jax.ShapeDtypeStruct((OWN, TOK), BF16),
            jax.ShapeDtypeStruct((36, TOK), BF16),
        ),
        in_specs=[anywhere] * 3,
        out_specs=[anywhere] * 3,
        scratch_shapes=[dma((3,))],
        name="write_out",
    )(lat, recon, out)
    return (lat[None], recon.T[None], out.T)


def solution(mesh):
    in_specs = (
        P("layer", "token", "latent"),
        P("layer", None),
        P("layer", None, "latent"),
        P("layer", "latent"),
        P("layer", "latent", None),
        P("latent", None),
        P("token", "latent"),
        P("latent"),
        P(None, ("layer", "latent")),
        P(None, ("layer", "latent")),
        P(("layer", "latent"), None),
    )
    out_specs = (
        P("layer", "token", "latent"),
        P("layer", "token", "latent"),
        P("token", ("layer", "latent")),
    )
    return jax.shard_map(
        per_device, mesh=mesh, in_specs=in_specs, out_specs=out_specs, check_vma=False
    )
```

time: 74 us -> 75.1 us (1.015)
  Pallas kernels: 68.7 us -> 74.3 us
  local copies, waits for them, and re-layouts: 4.39 us -> 0 us
    pallas_call x0 -> x1, Pallas kernels: none -> 10.8 us  [per_device(): pl.pallas_call(write_out, out_shape=(jax.ShapeDtypeStruct((TOK, LAT), BF1...]
    pallas_call x1, Pallas kernels: 68.7 us -> 63.5 us  [per_device(): pl.pallas_call(kernel, out_shape=(jax.ShapeDtypeStruct((TOK, LAT), BF16),...]
    unnamed x3 -> x0, local copies, waits for them, and re-layouts: 4.39 us -> none
where the time goes in v2:
time: 75.1 us; the launch traced here: 75 us
  Pallas kernels  74.3 us (99%)
    pallas_call x1, Pallas kernels, per_device(): pl.pallas_call(kernel, out_shape=(jax.ShapeDtypeStruct((TOK, LAT), BF16),...  63.5 us
    pallas_call x1, Pallas kernels, per_device(): pl.pallas_call(write_out, out_shape=(jax.ShapeDtypeStruct((TOK, LAT), BF1...  10.8 us

profile of v2, /device:TPU:1, one launch (start us, length us, event | category | flops | bytes accessed | tf_op | source)
XLA Modules:
  0.0 75.0 jit_solution(700938226094056497)
XLA Ops:
  0.6 63.5 %clt_mlp.1 = (bf16[256,512]{1,0:T(8,128)(2,1)}, bf16[72,256]{1,0:T(8,128)(2,1)}, bf16[36,256]{1,0:T(8,128)(2,1)}) custom-call(bf16[72,256]{1,0:T(8,128)(2,1)} %bitcast.18, f32[1,2304]{1,0:T(1,128)} %gain.1, f32[1,512]{1,0:T(1,128)} %encb.1, bf16[72,256]{1,0:T(8,128)(2,1)} %bitcast.19, f32[1,72]{1,0:T(1,128)} %bitcast.20, bf16[2304,512]{1,0:T(8,128)(2,1)} %bitcast.14, ...), custom_call_target="tpu_custom_call" | custom-call | flops 2000000000 | bytes 10000000 | tf_op jit(solution)/shard_map/clt_mlp/pallas_call | solution.py:422
  64.2 10.8 %write_out.1 = (bf16[256,512]{1,0:T(8,128)(2,1)}, bf16[72,256]{1,0:T(8,128)(2,1)}, bf16[36,256]{1,0:T(8,128)(2,1)}) custom-call(bf16[256,512]{1,0:T(8,128)(2,1)} %get-tuple-element.9.lat, bf16[72,256]{1,0:T(8,128)(2,1)} %get-tuple-element.10.recon, bf16[36,256]{1,0:T(8,128)(2,1)} %get-tuple-element.11.out), custom_call_target="tpu_custom_call" | custom-call | tf_op jit(solution)/shard_map/write_out/pallas_call | solution.py:456

commit v3 on v2

--- a/solution.py
+++ b/solution.py
@@ -57,7 +57,10 @@
 
     sibling = {"latent": chip * 2 + 1 - core}
     across = {"layer": 1 - layer}
-    across_sib = {"layer": 1 - layer, "latent": chip * 2 + 1 - core}
+
+    def across_b(d):
+        return {"layer": 1 - layer, "latent": chip_at(0, d) * 2 + core}
+
     own_lanes = pl.ds(pl.multiple_of(core * HALF, HALF), HALF)
     sib_lanes = pl.ds(pl.multiple_of((1 - core) * HALF, HALF), HALF)
 
@@ -89,8 +92,8 @@
         copy.start()
 
     barrier = pltpu.get_barrier_semaphore()
-    peers = [sibling, across, across_sib]
-    peers += [along_a(d) for d in (1, 2, 3)] + [along_b(d) for d in (1, 2, 3)]
+    peers = [sibling, across]
+    peers += [f(d) for f in (along_a, along_b, across_b) for d in (1, 2, 3)]
     for dev in peers:
         pl.semaphore_signal(barrier, inc=1, device_id=dev, device_id_type=MESH)
     loads[0].wait()
@@ -185,10 +188,11 @@
     bias = encb_b[...]
     lat_v[...] = jnp.maximum(inv * pre + jnp.concatenate([bias, bias], axis=1), 0.0).astype(BF16)
 
-    def project(dec_ref, i):
+    def project(dec_ref, i, base=None):
         for k in range(6):
             cols = slice(384 * k, 384 * (k + 1))
-            prod[i, cols, :] = lax.dot_general(dec_ref[:, cols], lat_v[...], TN, preferred_element_type=F32)
+            v = lax.dot_general(dec_ref[:, cols], lat_v[...], TN, preferred_element_type=F32)
+            prod[i, cols, :] = v if base is None else v + prod[base, cols, :]
 
     def whole_unit(i, c, lanes):
         rows = pl.ds(pl.multiple_of(c * CHIP, 16), CHIP)
@@ -241,44 +245,30 @@
 
     @pl.when(layer == 0)
     def _():
-        project(dec_n_v, 1)
-        hand_over(1, whole_unit)
         project(dec_s_v, 0)
+        project(dec_n_v, 1, base=0)
+
+    @pl.when(layer == 1)
+    def _():
+        project(dec_s_v, 1)
+
+    hand_over(1, whole_unit)
+
+    @pl.when(layer == 0)
+    def _():
         hand_over(0, whole_unit)
-        first_axis(1, whole_unit)
+
+    first_axis(1, whole_unit)
+    second_axis(1)
+
+    @pl.when(layer == 0)
+    def _():
         first_axis(0, whole_unit)
-        second_axis(1)
-        second_axis(0)
-        part = collect(1)
-        keep[1, 0] = part
-        z_send[1] = part.astype(BF16)
-        early = send(z_send.at[1], z_recv.at[1], ms_s.at[3], ms_r.at[3], across)
-        part = collect(0)
-        keep[0, 0] = part
-        z_send[0] = part.astype(BF16)
-        last = send(z_send.at[0], z_recv.at[0], ms_s.at[2], ms_r.at[2], across)
-        arrived(z_recv.at[0], ms_r.at[2])
-        keep[0, 1] = keep[1, 0] + z_recv[0].astype(F32)
-        all_sent(land.at[1, 0:31], rs_s.at[1])
-        all_sent(land.at[0, 0:31], rs_s.at[0])
-        settle([early, last])
-
-    @pl.when(layer == 1)
-    def _():
-        project(dec_s_v, 0)
-        hand_over(0, whole_unit)
-        first_axis(0, whole_unit)
-        second_axis(0)
-        part = collect(0)
-        z_send[0] = part.astype(BF16)
-        last = send(z_send.at[0], z_recv.at[0], ms_s.at[2], ms_r.at[2], across)
-        arrived(z_recv.at[1], ms_r.at[3])
-        keep[0, 0] = part + z_recv[1].astype(F32)
-        arrived(z_recv.at[0], ms_r.at[2])
-        keep[0, 1] = z_recv[0].astype(F32)
-        all_sent(land.at[0, 0:31], rs_s.at[0])
-        settle([last])
-
+
+    part = collect(1)
+    z_send[0] = part.astype(BF16)
+    sends.append(send(z_send.at[0], z_recv.at[0], ms_s.at[2], ms_r.at[2], across))
+    keep[1, 0] = part
     arrived(mg_recv, ms_r.at[0])
     arrived(fz_recv, ms_r.at[1])
     mine = frozen_v[:, own_lanes].astype(F32)
@@ -286,7 +276,8 @@
     fz = jnp.concatenate([jnp.where(first, mine, theirs), jnp.where(first, theirs, mine)], axis=0)
     mg0, mg1 = mg_send[...], mg_recv[...]
     mg = jnp.concatenate([jnp.where(first, mg0, mg1), jnp.where(first, mg1, mg0)], axis=0)
-    mixed = fz + keep[0, 0] + keep[0, 1]
+    arrived(z_recv.at[0], ms_r.at[2])
+    mixed = fz + keep[1, 0] + z_recv[0].astype(F32)
 
     sq_a[0] = jnp.broadcast_to(jnp.sum(mixed * mixed, axis=0, keepdims=True), (8, HALF))
 
@@ -315,12 +306,6 @@
         push2(0, 0, 0, d)
     share2(0, 0, 0)
 
-    rows_own = keep[0, 0]
-    low, high = rows_own[0:OWN], rows_own[OWN:CHIP]
-    rc_send[0:OWN, :] = jnp.where(first, high, low).astype(BF16)
-    rc_send[OWN:PAD, :] = jnp.zeros((PAD - OWN, HALF), BF16)
-    sends2.append(send(rc_send, rc_recv, ms_s.at[4], ms_r.at[4], sibling))
-    recon_v[:, own_lanes] = jnp.where(first, low, high).astype(BF16)
     lat_t[...] = lat_v[...].T
     lat_copy = pltpu.make_async_copy(lat_t, lat_out, in_sem.at[0])
     lat_copy.start()
@@ -330,6 +315,11 @@
         for d in (2, 1, 3):
             push2(a, b, 0, d)
         share2(a, b, a)
+
+    @pl.when(layer == 0)
+    def _():
+        second_axis(0)
+
     arrived(sq_a.at[1:4], sq_r.at[0])
     sq = sq_a[0] + sq_a[1] + sq_a[2] + sq_a[3]
     sq_b[0] = sq
@@ -338,10 +328,6 @@
     arrived(three, ag_r.at[1, 3])
     for a, b in SINGLES_B:
         share2(a, b, 4)
-    arrived(rc_recv, ms_r.at[4])
-    recon_v[:, sib_lanes] = rc_recv[0:OWN, :]
-    recon_copy = pltpu.make_async_copy(recon_v, recon_out, in_sem.at[1])
-    recon_copy.start()
     arrived(sq_b.at[1:4], sq_r.at[1])
     sq = sq_b[0] + sq_b[1] + sq_b[2] + sq_b[3]
     sq_d[0] = sq
@@ -354,6 +340,7 @@
     other = sq_d[1]
     both = jnp.concatenate([jnp.where(first, sq, other), jnp.where(first, other, sq)], axis=1)[0:1]
     scale = lax.rsqrt(both / D + EPS)
+
     for copy in loads[8:11]:
         copy.wait()
     for k in range(4):
@@ -368,33 +355,71 @@
         cols = slice(384 * k, 384 * (k + 1))
         prod[2, cols, :] = lax.dot_general(wd_v[:, cols], hidden, TN, preferred_element_type=F32)
     hand_over(2, split_unit)
+
+    @pl.when(layer == 0)
+    def _():
+        own = collect(0)
+        z_send[1] = (keep[1, 0] - own).astype(BF16)
+        send(z_send.at[1], z_recv.at[1], ms_s.at[3], ms_r.at[3], across)
+        keep[1, 0] = own
+
     first_axis(2, split_unit)
-    second_axis(2)
-    part = collect(2)
-    low, high = part[0:OWN], part[OWN:CHIP]
-    here = jnp.where(layer == 0, low, high)
-    there = jnp.where(layer == 0, high, low)
+
     zero = jnp.zeros((PAD - OWN, HALF), BF16)
-    fin_send[1, 0:OWN, :] = there.astype(BF16)
-    fin_send[1, OWN:PAD, :] = zero
-    sends2.append(send(fin_send.at[1], fin_recv.at[1], ms_s.at[5], ms_r.at[5], across_sib))
-    sends2.append(send(fin_send.at[1], fin_recv.at[2], ms_s.at[6], ms_r.at[6], across))
-    fin_send[0, 0:OWN, :] = here.astype(BF16)
-    fin_send[0, OWN:PAD, :] = zero
-    sends2.append(send(fin_send.at[0], fin_recv.at[0], ms_s.at[7], ms_r.at[7], sibling))
-    arrived(fin_recv.at[0], ms_r.at[7])
-    arrived(fin_recv.at[2], ms_r.at[6])
-    arrived(fin_recv.at[1], ms_r.at[5])
-    own_half = here + fin_recv[2, 0:OWN, :].astype(F32)
-    sib_half = fin_recv[0, 0:OWN, :].astype(F32) + fin_recv[1, 0:OWN, :].astype(F32)
-    out_v[:, own_lanes] = jnp.where(first, own_half[0:36], own_half[36:72]).astype(BF16)
+
+    for b in (2, 1, 3, 0):
+        at = 16 + 3 * b
+        arrived(land.at[2, at:at + 3], rs_1.at[2, b])
+        v = keep[2, b] + land[2, at].astype(F32) + land[2, at + 1].astype(F32) + land[2, at + 2].astype(F32)
+        low, high = v[0:OWN], v[OWN:CHIP]
+        here = jnp.where(layer == 0, low, high)
+        there = jnp.where(layer == 0, high, low)
+        fin_send[b, 0:OWN, :] = there.astype(BF16)
+        fin_send[b, OWN:PAD, :] = zero
+        send(fin_send.at[b], fin_recv.at[(4 - b) % 4], rs_s.at[3], rs_2.at[2], across_b(b) if b else across)
+        if b:
+            fin_send[3 + b, 0:OWN, :] = here.astype(BF16)
+            fin_send[3 + b, OWN:PAD, :] = zero
+            send(fin_send.at[3 + b], fin_recv.at[7 - b], rs_s.at[3], rs_2.at[2], along_b(b))
+
+    @pl.when(layer == 1)
+    def _():
+        arrived(z_recv.at[1], ms_r.at[3])
+        keep[1, 0] = keep[1, 0] + z_recv[1].astype(F32)
+
+    low, high = keep[1, 0, 0:OWN, :], keep[1, 0, OWN:CHIP, :]
+    rc_send[0:OWN, :] = jnp.where(first, high, low).astype(BF16)
+    rc_send[OWN:PAD, :] = zero
+    sends2.append(send(rc_send, rc_recv, ms_s.at[4], ms_r.at[4], sibling))
+    recon_v[:, own_lanes] = jnp.where(first, low, high).astype(BF16)
+    arrived(fin_recv.at[0:7], rs_2.at[2])
+    for k in range(7):
+        here = here + fin_recv[k, 0:OWN, :].astype(F32)
+    fin_send[7, 0:OWN, :] = here.astype(BF16)
+    fin_send[7, OWN:PAD, :] = zero
+    sends2.append(send(fin_send.at[7], fin_recv.at[7], ms_s.at[5], ms_r.at[5], sibling))
+    out_v[:, own_lanes] = jnp.where(first, here[0:36], here[36:72]).astype(BF16)
+    arrived(rc_recv, ms_r.at[4])
+    recon_v[:, sib_lanes] = rc_recv[0:OWN, :]
+    recon_copy = pltpu.make_async_copy(recon_v, recon_out, in_sem.at[1])
+    recon_copy.start()
+    arrived(fin_recv.at[7], ms_r.at[5])
+    sib_half = fin_recv[7, 0:OWN, :].astype(F32)
     out_v[:, sib_lanes] = jnp.where(first, sib_half[0:36], sib_half[36:72]).astype(BF16)
     out_copy = pltpu.make_async_copy(out_v, mlp_out, in_sem.at[2])
     out_copy.start()
     all_sent(lb.at[0:31], out_sem.at[0])
     all_sent(land.at[0, 0:31], out_sem.at[1])
     all_sent(sq_all, out_sem.at[2])
-    all_sent(land.at[2, 0:31], rs_s.at[2])
+    all_sent(land.at[1, 0:31], rs_s.at[1])
+    all_sent(land.at[2, 0:28], rs_s.at[2])
+    all_sent(fin_send.at[0:7], rs_s.at[3])
+
+    @pl.when(layer == 0)
+    def _():
+        all_sent(land.at[0, 0:31], rs_s.at[0])
+        all_sent(z_send.at[1], ms_s.at[3])
+
     settle(sends)
     settle(sends2)
     lat_copy.wait()
@@ -402,15 +427,10 @@
     out_copy.wait()
 
 
-def write_out(lat, recon, out, lat_out, recon_out, mlp_out, sem):
-    copies = [
-        pltpu.make_async_copy(src, dst, sem.at[i])
-        for i, (src, dst) in enumerate([(lat, lat_out), (recon, recon_out), (out, mlp_out)])
-    ]
-    for copy in copies:
-        copy.start()
-    for copy in copies:
-        copy.wait()
+def write_out(lat, recon, out, lat_out, recon_out, mlp_out):
+    lat_out[...] = lat[...]
+    recon_out[...] = recon[...]
+    mlp_out[...] = out[...]
 
 
 def per_device(
@@ -440,9 +460,9 @@
             vm((2, CHIP, HALF), BF16), vm((2, CHIP, HALF), BF16), vm((PAD, HALF), BF16), vm((PAD, HALF), BF16),
             vm((OWN, TOK), BF16),
             vm((7, 8, HALF), F32), vm((4, 8, HALF), F32), vm((4, 8, HALF), F32), vm((2, 8, HALF), F32), vm((D, TOK), BF16),
-            vm((2, PAD, HALF), BF16), vm((3, PAD, HALF), BF16), vm((36, TOK), BF16),
+            vm((8, PAD, HALF), BF16), vm((8, PAD, HALF), BF16), vm((36, TOK), BF16),
             dma((11,)), dma((3,)), dma((2, 7)), dma((2, 8)),
-            dma((3,)), dma((3, 4)), dma((3, 4)), dma((3,)), dma((3,)), dma((8,)), dma((8,)),
+            dma((4,)), dma((3, 4)), dma((3, 4)), dma((3,)), dma((3,)), dma((6,)), dma((6,)),
         ],
         compiler_params=pltpu.CompilerParams(
             collective_id=0, has_side_effects=True, vmem_limit_bytes=58 * 2**20
@@ -460,9 +480,8 @@
             jax.ShapeDtypeStruct((OWN, TOK), BF16),
             jax.ShapeDtypeStruct((36, TOK), BF16),
         ),
-        in_specs=[anywhere] * 3,
-        out_specs=[anywhere] * 3,
-        scratch_shapes=[dma((3,))],
+        in_specs=[pl.BlockSpec(memory_space=pltpu.VMEM)] * 3,
+        out_specs=[pl.BlockSpec(memory_space=pltpu.VMEM)] * 3,
         name="write_out",
     )(lat, recon, out)
     return (lat[None], recon.T[None], out.T)

time: 75.1 us -> 63.1 us (0.84)
  Pallas kernels: 74.3 us -> 62.4 us
    pallas_call x1, Pallas kernels: 10.8 us -> 1.7 us  [per_device(): pl.pallas_call(write_out, out_shape=(jax.ShapeDtypeStruct((TOK, LAT), BF1...]
    pallas_call x1, Pallas kernels: 63.5 us -> 60.7 us  [per_device(): pl.pallas_call(kernel, out_shape=(jax.ShapeDtypeStruct((TOK, LAT), BF16),...]
where the time goes in v3:
time: 63.1 us; the launch traced here: 63 us
  Pallas kernels  62.4 us (99%)
  between operations  0.64 us (1%)
    pallas_call x1, Pallas kernels, per_device(): pl.pallas_call(kernel, out_shape=(jax.ShapeDtypeStruct((TOK, LAT), BF16),...  60.7 us
    pallas_call x1, Pallas kernels, per_device(): pl.pallas_call(write_out, out_shape=(jax.ShapeDtypeStruct((TOK, LAT), BF1...  1.7 us

profile of v3, /device:TPU:1, one launch (start us, length us, event | category | flops | bytes accessed | tf_op | source)
XLA Modules:
  0.0 63.0 jit_solution(1978770061735656131)
XLA Ops:
  0.6 60.7 %clt_mlp.1 = (bf16[256,512]{1,0:T(8,128)(2,1)}, bf16[72,256]{1,0:T(8,128)(2,1)}, bf16[36,256]{1,0:T(8,128)(2,1)}) custom-call(bf16[72,256]{1,0:T(8,128)(2,1)} %bitcast.18, f32[1,2304]{1,0:T(1,128)} %gain.1, f32[1,512]{1,0:T(1,128)} %encb.1, bf16[72,256]{1,0:T(8,128)(2,1)} %bitcast.19, f32[1,72]{1,0:T(1,128)} %bitcast.20, bf16[2304,512]{1,0:T(8,128)(2,1)} %bitcast.14, ...), custom_call_target="tpu_custom_call" | custom-call | flops 2000000000 | bytes 10000000 | tf_op jit(solution)/shard_map/clt_mlp/pallas_call | solution.py:442
  61.3 1.7 %write_out.1 = (bf16[256,512]{1,0:T(8,128)(2,1)}, bf16[72,256]{1,0:T(8,128)(2,1)}, bf16[36,256]{1,0:T(8,128)(2,1)}) custom-call(bf16[256,512]{1,0:T(8,128)(2,1)} %get-tuple-element.9.lat, bf16[72,256]{1,0:T(8,128)(2,1)} %get-tuple-element.10.recon, bf16[36,256]{1,0:T(8,128)(2,1)} %get-tuple-element.11.out), custom_call_target="tpu_custom_call" | custom-call | tf_op jit(solution)/shard_map/write_out/pallas_call | solution.py:476

commit v4 on v3

--- a/solution.py
+++ b/solution.py
@@ -34,7 +34,7 @@
     prod, ys, land, keep, s1, s2,
     z_send, z_recv, rc_send, rc_recv, recon_v,
     sq_all, sq_a, sq_b, sq_d, g2, fin_send, fin_recv, out_v,
-    in_sem, out_sem, ag_r, ag_d, rs_s, rs_d, rs_1, rs_2, sq_r, ms_s, ms_r,
+    in_sem, out_sem, ag_r, ag_d, rs_s, rs_d, rs_1, rs_2, rs_x, sq_r, ms_s, ms_r,
 ):
     layer = lax.axis_index("layer")
     q = lax.axis_index("latent")
@@ -171,12 +171,25 @@
         shared(a, b, 1, a)
     for a, b in SINGLES_B:
         use(a, b)
-    for a in (1, 3, 2):
+
+    loads[6].wait()
+    loads[7].wait()
+
+    @pl.when(layer == 0)
+    def _():
+        dec_n_v[...] = dec_n_v[...] + dec_s_v[...]
+
+    for a in (1, 3):
         arrived(lb.at[pl.ds(core * 16 + slot(a, 1), 3)], ag_r.at[0, 3 + a])
         share(a, 1, 3, 4 + a)
-    for a in (1, 3, 2):
+    for a in (1, 3):
         shared(a, 1, 3, 4 + a)
-    for a, b in DIAGONALS:
+    for a, b in DIAGONALS[:4]:
+        use(a, b)
+    arrived(lb.at[pl.ds(core * 16 + slot(2, 1), 3)], ag_r.at[0, 5])
+    share(2, 1, 3, 6)
+    shared(2, 1, 3, 6)
+    for a, b in DIAGONALS[4:]:
         use(a, b)
     total = squares[0]
     for s in squares[1:]:
@@ -188,11 +201,10 @@
     bias = encb_b[...]
     lat_v[...] = jnp.maximum(inv * pre + jnp.concatenate([bias, bias], axis=1), 0.0).astype(BF16)
 
-    def project(dec_ref, i, base=None):
+    def project(dec_ref, i):
         for k in range(6):
             cols = slice(384 * k, 384 * (k + 1))
-            v = lax.dot_general(dec_ref[:, cols], lat_v[...], TN, preferred_element_type=F32)
-            prod[i, cols, :] = v if base is None else v + prod[base, cols, :]
+            prod[i, cols, :] = lax.dot_general(dec_ref[:, cols], lat_v[...], TN, preferred_element_type=F32)
 
     def whole_unit(i, c, lanes):
         rows = pl.ds(pl.multiple_of(c * CHIP, 16), CHIP)
@@ -204,16 +216,16 @@
         return jnp.concatenate([prod[i, low, lanes], prod[i, high, lanes]], axis=0)
 
     def hand_over(i, unit):
-        for a in (2, 1, 3, 0):
-            for b in range(4):
-                ys[i, slot(a, b)] = unit(i, chip_at(b, a), sib_lanes).astype(BF16)
-            send(ys.at[i, 4 * a:4 * a + 4], land.at[i, 4 * a:4 * a + 4], rs_s.at[i], rs_d.at[i, a], sibling)
+        for b in (2, 1, 3, 0):
+            for a in range(4):
+                ys[i, 4 * b + a] = unit(i, chip_at(b, a), sib_lanes).astype(BF16)
+            send(ys.at[i, 4 * b:4 * b + 4], land.at[i, 4 * b:4 * b + 4], rs_s.at[i], rs_d.at[i, b], sibling)
 
     def first_axis(i, unit):
-        for a in (2, 1, 3, 0):
-            arrived(land.at[i, 4 * a:4 * a + 4], rs_d.at[i, a])
-            for b in (2, 1, 3, 0):
-                s = slot(a, b)
+        for b in (2, 1, 3, 0):
+            arrived(land.at[i, 4 * b:4 * b + 4], rs_d.at[i, b])
+            for a in (2, 1, 3, 0):
+                s = 4 * b + a
                 v = unit(i, chip_at(a, b), own_lanes) + land[i, s].astype(F32)
                 if a:
                     s1[i, s] = v.astype(BF16)
@@ -221,13 +233,20 @@
                 else:
                     keep[i, b] = v
 
-    def second_axis(i):
+    def line_sum(i, b):
+        at = 16 + 3 * b
+        arrived(land.at[i, at:at + 3], rs_1.at[i, b])
+        return keep[i, b] + land[i, at].astype(F32) + land[i, at + 1].astype(F32) + land[i, at + 2].astype(F32)
+
+    def second_axis(i, both_layers):
         for b in (2, 1, 3, 0):
-            at = 16 + 3 * b
-            arrived(land.at[i, at:at + 3], rs_1.at[i, b])
-            v = keep[i, b] + land[i, at].astype(F32) + land[i, at + 1].astype(F32) + land[i, at + 2].astype(F32)
+            v = line_sum(i, b)
+            if b or both_layers:
+                s2[i, b] = v.astype(BF16)
+            if both_layers:
+                dev = across_b(b) if b else across
+                send(s2.at[i, b], land.at[i, 31 + (4 - b) % 4], rs_s.at[i], rs_x.at[0], dev)
             if b:
-                s2[i, b] = v.astype(BF16)
                 send(s2.at[i, b], land.at[i, 28 + 3 - b], rs_s.at[i], rs_2.at[i], along_b(b))
             else:
                 keep[i, 0] = v
@@ -240,35 +259,28 @@
         for copy in copies:
             copy.wait_send()
 
-    loads[6].wait()
-    loads[7].wait()
+    @pl.when(layer == 0)
+    def _():
+        project(dec_n_v, 1)
+
+    @pl.when(layer == 1)
+    def _():
+        project(dec_s_v, 1)
+
+    hand_over(1, whole_unit)
 
     @pl.when(layer == 0)
     def _():
         project(dec_s_v, 0)
-        project(dec_n_v, 1, base=0)
-
-    @pl.when(layer == 1)
-    def _():
-        project(dec_s_v, 1)
-
-    hand_over(1, whole_unit)
-
-    @pl.when(layer == 0)
-    def _():
         hand_over(0, whole_unit)
 
     first_axis(1, whole_unit)
-    second_axis(1)
+    second_axis(1, True)
 
     @pl.when(layer == 0)
     def _():
         first_axis(0, whole_unit)
 
-    part = collect(1)
-    z_send[0] = part.astype(BF16)
-    sends.append(send(z_send.at[0], z_recv.at[0], ms_s.at[2], ms_r.at[2], across))
-    keep[1, 0] = part
     arrived(mg_recv, ms_r.at[0])
     arrived(fz_recv, ms_r.at[1])
     mine = frozen_v[:, own_lanes].astype(F32)
@@ -276,8 +288,11 @@
     fz = jnp.concatenate([jnp.where(first, mine, theirs), jnp.where(first, theirs, mine)], axis=0)
     mg0, mg1 = mg_send[...], mg_recv[...]
     mg = jnp.concatenate([jnp.where(first, mg0, mg1), jnp.where(first, mg1, mg0)], axis=0)
-    arrived(z_recv.at[0], ms_r.at[2])
-    mixed = fz + keep[1, 0] + z_recv[0].astype(F32)
+    part = collect(1)
+    keep[1, 0] = part
+    arrived(land.at[1, 31:35], rs_x.at[0])
+    other = land[1, 31].astype(F32) + land[1, 32].astype(F32) + land[1, 33].astype(F32) + land[1, 34].astype(F32)
+    mixed = fz + part + other
 
     sq_a[0] = jnp.broadcast_to(jnp.sum(mixed * mixed, axis=0, keepdims=True), (8, HALF))
 
@@ -318,7 +333,7 @@
 
     @pl.when(layer == 0)
     def _():
-        second_axis(0)
+        second_axis(0, False)
 
     arrived(sq_a.at[1:4], sq_r.at[0])
     sq = sq_a[0] + sq_a[1] + sq_a[2] + sq_a[3]
@@ -337,8 +352,8 @@
         for b in (1, 3, 2):
             share2(a, b, 4 + a)
     arrived(sq_d.at[1], sq_r.at[2])
-    other = sq_d[1]
-    both = jnp.concatenate([jnp.where(first, sq, other), jnp.where(first, other, sq)], axis=1)[0:1]
+    sq_sib = sq_d[1]
+    both = jnp.concatenate([jnp.where(first, sq, sq_sib), jnp.where(first, sq_sib, sq)], axis=1)[0:1]
     scale = lax.rsqrt(both / D + EPS)
 
     for copy in loads[8:11]:
@@ -359,8 +374,8 @@
     @pl.when(layer == 0)
     def _():
         own = collect(0)
-        z_send[1] = (keep[1, 0] - own).astype(BF16)
-        send(z_send.at[1], z_recv.at[1], ms_s.at[3], ms_r.at[3], across)
+        z_send[...] = (keep[1, 0] - own).astype(BF16)
+        send(z_send, z_recv, ms_s.at[3], ms_r.at[3], across)
         keep[1, 0] = own
 
     first_axis(2, split_unit)
@@ -368,9 +383,7 @@
     zero = jnp.zeros((PAD - OWN, HALF), BF16)
 
     for b in (2, 1, 3, 0):
-        at = 16 + 3 * b
-        arrived(land.at[2, at:at + 3], rs_1.at[2, b])
-        v = keep[2, b] + land[2, at].astype(F32) + land[2, at + 1].astype(F32) + land[2, at + 2].astype(F32)
+        v = line_sum(2, b)
         low, high = v[0:OWN], v[OWN:CHIP]
         here = jnp.where(layer == 0, low, high)
         there = jnp.where(layer == 0, high, low)
@@ -384,8 +397,8 @@
 
     @pl.when(layer == 1)
     def _():
-        arrived(z_recv.at[1], ms_r.at[3])
-        keep[1, 0] = keep[1, 0] + z_recv[1].astype(F32)
+        arrived(z_recv, ms_r.at[3])
+        keep[1, 0] = keep[1, 0] + z_recv[...].astype(F32)
 
     low, high = keep[1, 0, 0:OWN, :], keep[1, 0, OWN:CHIP, :]
     rc_send[0:OWN, :] = jnp.where(first, high, low).astype(BF16)
@@ -411,14 +424,14 @@
     all_sent(lb.at[0:31], out_sem.at[0])
     all_sent(land.at[0, 0:31], out_sem.at[1])
     all_sent(sq_all, out_sem.at[2])
-    all_sent(land.at[1, 0:31], rs_s.at[1])
+    all_sent(land.at[1, 0:35], rs_s.at[1])
     all_sent(land.at[2, 0:28], rs_s.at[2])
     all_sent(fin_send.at[0:7], rs_s.at[3])
 
     @pl.when(layer == 0)
     def _():
         all_sent(land.at[0, 0:31], rs_s.at[0])
-        all_sent(z_send.at[1], ms_s.at[3])
+        all_sent(z_send, ms_s.at[3])
 
     settle(sends)
     settle(sends2)
@@ -455,14 +468,14 @@
             vm((D, HALF), F32), vm((LAT, HALF), F32), vm((32, PAD, TOK), BF16), vm((D, TOK), BF16),
             vm((LAT, TOK), BF16), vm((TOK, LAT), BF16),
             vm((PAD, HALF), BF16), vm((PAD, HALF), BF16), vm((OWN, HALF), F32), vm((OWN, HALF), F32),
-            vm((3, D, TOK), F32), vm((3, 16, CHIP, HALF), BF16), vm((3, 31, CHIP, HALF), BF16),
+            vm((3, D, TOK), F32), vm((3, 16, CHIP, HALF), BF16), vm((3, 35, CHIP, HALF), BF16),
             vm((3, 4, CHIP, HALF), F32), vm((3, 16, CHIP, HALF), BF16), vm((3, 4, CHIP, HALF), BF16),
-            vm((2, CHIP, HALF), BF16), vm((2, CHIP, HALF), BF16), vm((PAD, HALF), BF16), vm((PAD, HALF), BF16),
+            vm((CHIP, HALF), BF16), vm((CHIP, HALF), BF16), vm((PAD, HALF), BF16), vm((PAD, HALF), BF16),
             vm((OWN, TOK), BF16),
             vm((7, 8, HALF), F32), vm((4, 8, HALF), F32), vm((4, 8, HALF), F32), vm((2, 8, HALF), F32), vm((D, TOK), BF16),
             vm((8, PAD, HALF), BF16), vm((8, PAD, HALF), BF16), vm((36, TOK), BF16),
             dma((11,)), dma((3,)), dma((2, 7)), dma((2, 8)),
-            dma((4,)), dma((3, 4)), dma((3, 4)), dma((3,)), dma((3,)), dma((6,)), dma((6,)),
+            dma((4,)), dma((3, 4)), dma((3, 4)), dma((3,)), dma((1,)), dma((3,)), dma((6,)), dma((6,)),
         ],
         compiler_params=pltpu.CompilerParams(
             collective_id=0, has_side_effects=True, vmem_limit_bytes=58 * 2**20

time: 63.1 us -> 60.7 us (0.962)
  Pallas kernels: 62.4 us -> 59.9 us
    pallas_call x1, Pallas kernels: 60.7 us -> 58.2 us  [per_device(): pl.pallas_call(kernel, out_shape=(jax.ShapeDtypeStruct((TOK, LAT), BF16),...]
where the time goes in v4:
time: 60.7 us; the launch traced here: 60.6 us
  Pallas kernels  59.9 us (99%)
  between operations  0.64 us (1%)
    pallas_call x1, Pallas kernels, per_device(): pl.pallas_call(kernel, out_shape=(jax.ShapeDtypeStruct((TOK, LAT), BF16),...  58.2 us
    pallas_call x1, Pallas kernels, per_device(): pl.pallas_call(write_out, out_shape=(jax.ShapeDtypeStruct((TOK, LAT), BF1...  1.7 us

profile of v4, /device:TPU:1, one launch (start us, length us, event | category | flops | bytes accessed | tf_op | source)
XLA Modules:
  0.0 60.6 jit_solution(8751154638838023775)
XLA Ops:
  0.6 58.2 %clt_mlp.1 = (bf16[256,512]{1,0:T(8,128)(2,1)}, bf16[72,256]{1,0:T(8,128)(2,1)}, bf16[36,256]{1,0:T(8,128)(2,1)}) custom-call(bf16[72,256]{1,0:T(8,128)(2,1)} %bitcast.18, f32[1,2304]{1,0:T(1,128)} %gain.1, f32[1,512]{1,0:T(1,128)} %encb.1, bf16[72,256]{1,0:T(8,128)(2,1)} %bitcast.19, f32[1,72]{1,0:T(1,128)} %bitcast.20, bf16[2304,512]{1,0:T(8,128)(2,1)} %bitcast.14, ...), custom_call_target="tpu_custom_call" | custom-call | flops 2000000000 | bytes 10000000 | tf_op jit(solution)/shard_map/clt_mlp/pallas_call | solution.py:455
  58.9 1.7 %write_out.1 = (bf16[256,512]{1,0:T(8,128)(2,1)}, bf16[72,256]{1,0:T(8,128)(2,1)}, bf16[36,256]{1,0:T(8,128)(2,1)}) custom-call(bf16[256,512]{1,0:T(8,128)(2,1)} %get-tuple-element.9.lat, bf16[72,256]{1,0:T(8,128)(2,1)} %get-tuple-element.10.recon, bf16[36,256]{1,0:T(8,128)(2,1)} %get-tuple-element.11.out), custom_call_target="tpu_custom_call" | custom-call | tf_op jit(solution)/shard_map/write_out/pallas_call | solution.py:489
